TPU v7x, 512 devices: a whole 4x8x8 slice. The times are simulated.
512 devices in a mesh: section: 32 (over x, y), expert: 16 (over z, core).
Axes of the slice: x: 4, y: 8, z: 8, core: 2. Of those that a mesh axis runs over, the one named last changes fastest.
Arguments:
- tokens: bfloat16 [32, 2048, 1024], P('section', 'expert'), may hold values from -6 to 6
- routes: int32 [32, 2048, 8], P('section'), may hold values from 0 to 15, all different within a row
- route_weight: float32 [32, 2048, 8], P('section'), may hold values from 0.1 to 1
- projections: bfloat16 [32, 16, 3, 1024, 384], P('section', 'expert'), may hold values from -0.91855865 to 0.91855865
Outputs:
- merged: bfloat16 [32, 16, 3, 1024, 192], P('section', 'expert')
- handed: bfloat16 [32, 2048, 1024], P('section', 'expert')
Inputs may be any that keep to these rules, and one draw needn't show every extreme that they name: `routes`: each token names 8 different experts of 0 to 15, and every one of them is named by some token of each layer.
All inputs are finite; a program needn't handle non-finite values.
Results may differ from a plain program's by a relative error of at most 0.02.
Values may be sent and summed in bfloat16 or wider, within the bound.
No kernel may reach another device: no remote copies, remote signals or barrier semaphores. Data moves between devices by JAX's collectives and lax.ppermute only.
A program may use at most 64 MiB of HBM per device.

v0:
```python
import jax
import jax.numpy as jnp
from jax import lax
from jax.sharding import PartitionSpec as P

EPS = 1e-06


def partner(array, axis, bit):
    return lax.ppermute(array, axis, [(i, i ^ 1 << bit) for i in range(lax.axis_size(axis))])


def shifted(block, axis, distance):
    devices = range(lax.axis_size(axis))
    route = [(i - distance, i) for i in devices if i - distance in devices]
    return lax.ppermute(block, axis, route)


def silu_mix(activations, gate_matrix, up_matrix):
    gate_out = jnp.dot(activations, gate_matrix, preferred_element_type=jnp.float32)
    up_out = jnp.dot(activations, up_matrix, preferred_element_type=jnp.float32)
    return (jax.nn.silu(gate_out) * up_out).astype(jnp.bfloat16)


def local(tokens, routes, route_weight, projections):
    x_local = tokens[0]
    layer_routes = routes[0]
    layer_weight = route_weight[0]
    weights = projections[0, 0]
    expert_count = lax.axis_size("expert")
    pair_count = expert_count // 2
    pair_bit = expert_count.bit_length() - 2
    device_index = lax.axis_index("expert")
    is_upper = device_index >= pair_count
    half_units = weights.shape[2] // 2
    own_start = jnp.where(is_upper, half_units, 0).astype(jnp.int32)
    other_start = half_units - own_start
    x_all = lax.all_gather(x_local, "expert", axis=0, tiled=True)
    hidden = silu_mix(x_all, weights[0], weights[1])
    mine_w = lax.dynamic_slice_in_dim(weights, own_start, half_units, 2)
    send_w = lax.dynamic_slice_in_dim(weights, other_start, half_units, 2)
    partner_w = partner(send_w, "expert", pair_bit)
    hidden_mine = lax.dynamic_slice_in_dim(hidden, own_start, half_units, 1)
    outgoing = lax.dynamic_slice_in_dim(hidden, other_start, half_units, 1)
    partner_hidden = partner(outgoing, "expert", pair_bit)
    lower_id = device_index % pair_count
    upper_id = lower_id + pair_count
    in_pair = (layer_routes == lower_id) | (layer_routes == upper_id)
    members = jnp.sum(in_pair.astype(jnp.float32), axis=1)
    pair_weight = jnp.sum(jnp.where(in_pair, layer_weight, jnp.float32(0.0)), axis=1)
    used_rows = jnp.maximum(jnp.sum(members), jnp.float32(1.0))
    mine_f = hidden_mine.astype(jnp.float32)
    partner_f = partner_hidden.astype(jnp.float32)
    selector = members[:, None]
    energy_mine = jnp.sum(selector * mine_f * mine_f, axis=0) / used_rows
    energy_partner = jnp.sum(selector * partner_f * partner_f, axis=0) / used_rows
    cross_term = jnp.sum(selector * mine_f * partner_f, axis=0) / used_rows
    energy_low = jnp.where(is_upper, energy_partner, energy_mine)
    energy_high = jnp.where(is_upper, energy_mine, energy_partner)
    agreement = 0.5 * (1.0 + cross_term / jnp.sqrt(energy_low * energy_high + EPS))
    root_low = jnp.sqrt(energy_low + EPS)
    root_high = jnp.sqrt(energy_high + EPS)
    blend = root_low / (root_low + agreement * root_high)
    low_proj = jnp.where(is_upper, partner_w, mine_w).astype(jnp.float32)
    high_proj = jnp.where(is_upper, mine_w, partner_w).astype(jnp.float32)
    merged_w = (blend * low_proj + (1.0 - blend) * high_proj).astype(jnp.bfloat16)
    inner = silu_mix(x_all, merged_w[0], merged_w[1])
    product = lax.dot_general(
        inner, merged_w[2], (((1,), (1,)), ((), ())), preferred_element_type=jnp.float32
    )
    layer_total = lax.psum_scatter(
        (pair_weight[:, None] * product).astype(jnp.bfloat16),
        "expert",
        scatter_dimension=0,
        tiled=True,
    ).astype(jnp.float32)
    block_out = (x_local.astype(jnp.float32) + layer_total).astype(jnp.bfloat16)
    handed = shifted(block_out, "section", 1)
    return (merged_w[None, None], handed[None])


def solution(mesh):
    in_specs = (
        P("section", "expert", None),
        P("section", None, None),
        P("section", None, None),
        P("section", "expert", None, None, None),
    )
    out_specs = (P("section", "expert", None, None, None), P("section", "expert", None))
    return jax.shard_map(local, mesh=mesh, in_specs=in_specs, out_specs=out_specs, check_vma=False)
```

profile of v0, /device:TPU:6, one launch (start us, length us, event | category | flops | bytes accessed | tf_op | source)
XLA Modules:
  0.0 257.6 jit_solution(3199247522294408720)
XLA Ops:
  7.2 0.0 all-gather.3.cloned.1.call-start
  7.2 0.7 all-gather.3.cloned.1.call-update
  7.9 0.0 reduce-scatter.2.cloned.1.call-start
  8.0 52.5 %all-gather.3.cloned.1.call-done = bf16[1,2048,1024]{2,1,0:T(8,128)(2,1)} async-done(((bf16[1,128,1024]{2,1,0:T(8,128)(2,1)}), bf16[1,2048,1024]{2,1,0:T(8,128)(2,1)}) %all-gather.3.cloned.1.call-update) | async-done | bytes 4194320 | tf_op jit(solution)/shard_map/all_gather | solution.py:38
  60.4 0.0 copy-start
  60.4 4.4 %fusion.6 = f32[2048,384]{0,1:T(8,128)S(1)} fusion(bf16[1,2048,1024]{2,1,0:T(8,128)(2,1)} %all-gather.3.cloned.1.call-done, bf16[1,1,3,1024,384]{4,3,2,1,0:T(8,128)(2,1)} %param.7), kind=kOutput, calls=%fused_computation.7 | convolution fusion | flops 1610612736 | bytes 8126464 | tf_op jit(solution)/shard_map/dot_general | solution.py:20
  64.9 0.0 copy-done
  64.9 0.0 copy-start.2
  64.9 3.8 %multiply_convert_fusion.1 = bf16[2048,384]{0,1:T(8,128)(2,1)S(1)} fusion(f32[2048,384]{0,1:T(8,128)S(1)} %fusion.6, bf16[1,2048,1024]{2,1,0:T(8,128)(2,1)S(1)} %copy-done, bf16[1,1,3,1024,384]{4,3,2,1,0:T(8,128)(2,1)} %param.7), kind=kOutput, calls=%fused_computation.9 | convolution fusion | flops 1615331328 | bytes 9699328 | tf_op jit(solution)/shard_map/dot_general | solution.py:21
  68.7 0.0 copy-start.4
  68.7 1.1 constant_dynamic-slice_fusion.2
  69.8 4.8 %collective-permute-start = (bf16[2048,192]{0,1:T(8,128)(2,1)}, bf16[2048,192]{0,1:T(8,128)(2,1)}, u32[]{:S(2)}, u32[]{:S(2)}) collective-permute-start(bf16[2048,192]{0,1:T(8,128)(2,1)} %constant_dynamic-slice_fusion.2), channel_id=1, source_target_pairs={{0,8},{1,9},{2,10},{3,11},{4,12},{5,13},{6,14},{7,15},{8,0},{9,1},... | collective-permute-start | bytes 2359304 | tf_op jit(solution)/shard_map/ppermute | solution.py:10
  74.6 0.0 copy-done.2
  74.6 1.6 constant_dynamic-slice_fusion
  76.2 0.0 copy-done.4
  76.2 0.0 copy-start.6
  76.2 0.0 copy-start.7
  76.2 1.5 copy.6
  77.7 5.1 %collective-permute-start.1 = (bf16[3,1024,192]{1,2,0:T(8,128)(2,1)}, bf16[3,1024,192]{1,2,0:T(8,128)(2,1)}, u32[]{:S(2)}, u32[]{:S(2)}) collective-permute-start(bf16[3,1024,192]{1,2,0:T(8,128)(2,1)} %bitcast.61), channel_id=1, source_target_pairs={{0,8},{1,9},{2,10},{3,11},{4,12},{5,13},{6,14},{7,15},{8,0},{9,1},... | collective-permute-start | bytes 3538952 | tf_op jit(solution)/shard_map/ppermute | solution.py:10
  82.9 0.7 copy.7
  83.6 0.0 copy-done.6
  83.6 0.0 copy-done.7
  83.6 0.6 select_reduce_fusion
  84.9 37.1 %collective-permute-done = bf16[2048,192]{0,1:T(8,128)(2,1)} collective-permute-done((bf16[2048,192]{0,1:T(8,128)(2,1)}, bf16[2048,192]{0,1:T(8,128)(2,1)}, u32[]{:S(2)}, u32[]{:S(2)}) %collective-permute-start) | collective-permute-done | bytes 786464 | tf_op jit(solution)/shard_map/ppermute | solution.py:10
  122.0 0.0 copy-start.1
  122.0 2.1 fusion.22
  124.2 39.1 %collective-permute-done.1 = bf16[3,1024,192]{1,2,0:T(8,128)(2,1)} collective-permute-done((bf16[3,1024,192]{1,2,0:T(8,128)(2,1)}, bf16[3,1024,192]{1,2,0:T(8,128)(2,1)}, u32[]{:S(2)}, u32[]{:S(2)}) %collective-permute-start.1) | collective-permute-done | bytes 1179680 | tf_op jit(solution)/shard_map/ppermute | solution.py:10
  163.3 2.0 add_convert_fusion
  165.2 0.0 copy-done.1
  165.2 0.0 copy-start.3
  165.3 1.5 fusion.10
  166.8 0.0 copy-done.3
  166.8 6.9 %multiply_convert_fusion = bf16[2048,1024]{1,0:T(8,128)(2,1)} fusion(f32[2048]{0:T(1024)S(1)} %get-tuple-element.5, bf16[1,2048,1024]{2,1,0:T(8,128)(2,1)} %all-gather.3.cloned.1.call-done, f32[2048,192]{0,1:T(8,128)S(1)} %fusion.10, bf16[3,1024,192]{1,2,0:T(8,128)(2,1)S(1)} %add_convert_fusion), kind=kOutput, calls=%fused_computation | convolution fusion | flops 1617166336 | bytes 10756096 | tf_op jit(solution)/shard_map/dot_general | solution.py:68
  173.7 0.0 copy-start.5
  173.7 0.0 reduce-scatter.2.cloned.1.call-update
  173.7 64.9 %reduce-scatter.2.cloned.1.call-done = bf16[128,1024]{1,0:T(8,128)(2,1)} async-done(((bf16[2048,1024]{1,0:T(8,128)(2,1)}), bf16[128,1024]{1,0:T(8,128)(2,1)}) %reduce-scatter.2.cloned.1.call-update) | async-done | bytes 262160 | tf_op jit(solution)/shard_map/reduce_scatter | solution.py:71
  238.6 0.0 copy-done.5
  238.6 1.0 fusion.32
  239.6 3.4 %collective-permute-start.2 = (bf16[128,1024]{1,0:T(8,128)(2,1)S(1)}, bf16[128,1024]{1,0:T(8,128)(2,1)S(1)}, u32[]{:S(2)}, u32[]{:S(2)}) collective-permute-start(bf16[128,1024]{1,0:T(8,128)(2,1)S(1)} %fusion.32), channel_id=1, source_target_pairs={{0,16},{16,32},{32,48},{48,64},{64,80},{80,96},{96,112},{112,128},... | collective-permute-start | bytes 786440 | tf_op jit(solution)/shard_map/ppermute | solution.py:16
  243.1 7.0 %collective-permute-done.2 = bf16[128,1024]{1,0:T(8,128)(2,1)S(1)} collective-permute-done((bf16[128,1024]{1,0:T(8,128)(2,1)S(1)}, bf16[128,1024]{1,0:T(8,128)(2,1)S(1)}, u32[]{:S(2)}, u32[]{:S(2)}) %collective-permute-start.2) | collective-permute-done | bytes 262176 | tf_op jit(solution)/shard_map/ppermute | solution.py:16
  250.0 0.7 copy.9
  (1 shorter events, 0.0 us)
Async XLA Ops:
  7.2 53.3 %all-gather.3.cloned.1.call-start = ((), (), s32[]{:S(2)}) async-start(), calls=%async_computation.2 | async-start | bytes 4456448 | tf_op jit(solution)/shard_map/all_gather | solution.py:38
  7.9 230.7 %reduce-scatter.2.cloned.1.call-start = ((), (), s32[]{:S(2)}) async-start(), calls=%async_computation.1 | async-start | bytes 4456448 | tf_op jit(solution)/shard_map/reduce_scatter | solution.py:71
  60.4 4.4 %copy-start = (bf16[1,2048,1024]{2,1,0:T(8,128)(2,1)S(1)}, bf16[1,2048,1024]{2,1,0:T(8,128)(2,1)}, u32[]{:S(2)}) copy-start(bf16[1,2048,1024]{2,1,0:T(8,128)(2,1)} %all-gather.3.cloned.1.call-done) | copy-start | bytes 12582916
  64.9 9.7 %copy-start.2 = (bf16[1,1,3,1024,384]{4,3,2,1,0:T(8,128)(2,1)S(1)}, bf16[1,1,3,1024,384]{4,3,2,1,0:T(8,128)(2,1)}, u32[]{:S(2)}) copy-start(bf16[1,1,3,1024,384]{4,3,2,1,0:T(8,128)(2,1)} %param.7) | copy-start | bytes 7077892
  68.7 7.5 %copy-start.4 = (bf16[2048,384]{0,1:T(8,128)(2,1)}, bf16[2048,384]{0,1:T(8,128)(2,1)S(1)}, u32[]{:S(2)}) copy-start(bf16[2048,384]{0,1:T(8,128)(2,1)S(1)} %multiply_convert_fusion.1) | copy-start | bytes 4718596
  69.8 52.2 %collective-permute-start = (bf16[2048,192]{0,1:T(8,128)(2,1)}, bf16[2048,192]{0,1:T(8,128)(2,1)}, u32[]{:S(2)}, u32[]{:S(2)}) collective-permute-start(bf16[2048,192]{0,1:T(8,128)(2,1)} %constant_dynamic-slice_fusion.2), channel_id=1, source_target_pairs={{0,8},{1,9},{2,10},{3,11},{4,12},{5,13},{6,14},{7,15},{8,0},{9,1},... | collective-permute-start | bytes 2359304 | tf_op jit(solution)/shard_map/ppermute | solution.py:10
  76.2 7.4 %copy-start.6 = (f32[1,2048,8]{1,2,0:T(8,128)S(1)}, f32[1,2048,8]{1,2,0:T(8,128)}, u32[]{:S(2)}) copy-start(f32[1,2048,8]{1,2,0:T(8,128)} %param.6) | copy-start | bytes 196612
  76.2 7.4 %copy-start.7 = (s32[1,2048,8]{1,2,0:T(8,128)S(1)}, s32[1,2048,8]{1,2,0:T(8,128)}, u32[]{:S(2)}) copy-start(s32[1,2048,8]{1,2,0:T(8,128)} %param.5) | copy-start | bytes 196612
  77.7 85.5 %collective-permute-start.1 = (bf16[3,1024,192]{1,2,0:T(8,128)(2,1)}, bf16[3,1024,192]{1,2,0:T(8,128)(2,1)}, u32[]{:S(2)}, u32[]{:S(2)}) collective-permute-start(bf16[3,1024,192]{1,2,0:T(8,128)(2,1)} %bitcast.61), channel_id=1, source_target_pairs={{0,8},{1,9},{2,10},{3,11},{4,12},{5,13},{6,14},{7,15},{8,0},{9,1},... | collective-permute-start | bytes 3538952 | tf_op jit(solution)/shard_map/ppermute | solution.py:10
  122.0 43.2 %copy-start.1 = (bf16[1,2048,1024]{2,1,0:T(8,128)(2,1)S(1)}, bf16[1,2048,1024]{2,1,0:T(8,128)(2,1)}, u32[]{:S(2)}) copy-start(bf16[1,2048,1024]{2,1,0:T(8,128)(2,1)} %all-gather.3.cloned.1.call-done) | copy-start | bytes 12582916
  165.2 1.5 copy-start.3
  173.7 64.9 %copy-start.5 = (bf16[1,128,1024]{2,1,0:T(8,128)(2,1)S(1)}, bf16[1,128,1024]{2,1,0:T(8,128)(2,1)}, u32[]{:S(2)}) copy-start(bf16[1,128,1024]{2,1,0:T(8,128)(2,1)} %param.4) | copy-start | bytes 786436
  239.6 10.4 %collective-permute-start.2 = (bf16[128,1024]{1,0:T(8,128)(2,1)S(1)}, bf16[128,1024]{1,0:T(8,128)(2,1)S(1)}, u32[]{:S(2)}, u32[]{:S(2)}) collective-permute-start(bf16[128,1024]{1,0:T(8,128)(2,1)S(1)} %fusion.32), channel_id=1, source_target_pairs={{0,16},{16,32},{32,48},{48,64},{64,80},{80,96},{96,112},{112,128},... | collective-permute-start | bytes 786440 | tf_op jit(solution)/shard_map/ppermute | solution.py:16
Sparse Core Ops, SparseCore 0:
  10.1 50.2 all-gather.2
  173.9 64.7 reduce-scatter.1
where the time goes:
time: 258 us
  waiting for transfers between devices  201 us (78%)
  matrix products  16.7 us (6%)
  between operations  14.9 us (6%)
  starting transfers between devices  13.4 us (5%)
  other arithmetic  5.79 us (2%)
  local copies, waits for them, and re-layouts  5.62 us (2%)
    ppermute x2, waiting for transfers between devices, partner(): lax.ppermute(array, axis, [(i, i ^ 1 << bit) for i in range(lax.axis_size...  76.2 us
    reduce_scatter x1, waiting for transfers between devices, local(): lax.psum_scatter((pair_weight[:, None] * product).astype(jnp.bfloat16), '...  64.9 us
    all_gather x1, waiting for transfers between devices, local(): x_all = lax.all_gather(x_local, 'expert', axis=0, tiled=True)  52.5 us
    ppermute x2, starting transfers between devices, partner(): lax.ppermute(array, axis, [(i, i ^ 1 << bit) for i in range(lax.axis_size...  9.9 us
    ppermute x1, waiting for transfers between devices, shifted(): return lax.ppermute(block, axis, route)  6.97 us
    dot_general x1, matrix products, local(): lax.dot_general(inner, merged_w[2], (((1,), (1,)), ((), ())), preferred_e...  6.91 us
    dot_general x2, matrix products, silu_mix(): jnp.dot(activations, gate_matrix, preferred_element_type=jnp.float32)  5.97 us
  transfers between devices with their start and end apart: 5, of which 5 were waited for; matrix products, arithmetic and copies ran while one was open for 3% of the time, Pallas kernels for 0%

commit v1 on v0

v1 whole, which is shorter than its diff:
```python
import jax
import jax.numpy as jnp
from jax import lax
from jax.sharding import PartitionSpec as P

EPS = 1e-06
CORES = 2


def along(array, count, target):
    return lax.ppermute(array, "expert", [(i, target(i)) for i in range(count)])


def ring(count, steps):
    return lambda i: (i + CORES * steps) % count


def next_layer(array, target):
    layers, count = lax.axis_size("section"), lax.axis_size("expert")
    route = [
        (layer * count + i, (layer + 1) * count + target(i))
        for layer in range(layers - 1)
        for i in range(count)
    ]
    return lax.ppermute(array, ("section", "expert"), route)


def against(activations, matrix):
    return lax.dot_general(
        activations, matrix, (((1,), (1,)), ((), ())), preferred_element_type=jnp.float32
    )


def silu_mix(activations, gate_matrix, up_matrix):
    return jax.nn.silu(against(activations, gate_matrix)) * against(activations, up_matrix)


def local(tokens, routes, route_weight, projections):
    x_local = tokens[0]
    layer_routes = routes[0]
    layer_weight = route_weight[0]
    weights = jnp.swapaxes(projections[0, 0], 1, 2)
    count = lax.axis_size("expert")
    pair_count = count // 2
    chips = count // CORES
    me = lax.axis_index("expert")
    chip, core = me // CORES, me % CORES
    is_upper = me >= pair_count
    half_units = weights.shape[1] // 2
    own_start = jnp.where(is_upper, half_units, 0).astype(jnp.int32)
    other_start = half_units - own_start
    rows = x_local.shape[0]

    mine_w = lax.dynamic_slice_in_dim(weights, own_start, half_units, 1)
    send_w = lax.dynamic_slice_in_dim(weights, other_start, half_units, 1)
    across = lambda i: (i + pair_count) % count
    partner_in = along(send_w[:2], count, across)
    send_down, partner_in = lax.optimization_barrier((send_w[2], partner_in))
    partner_down = along(send_down, count, across)
    x_all = lax.all_gather(x_local, "expert", axis=0, tiled=True)

    lower_id = me % pair_count

    def routed(pair):
        return (layer_routes == pair) | (layer_routes == pair + pair_count)

    def weight_of(pair):
        return jnp.sum(jnp.where(routed(pair), layer_weight, jnp.float32(0.0)), axis=1)

    members = jnp.sum(routed(lower_id).astype(jnp.float32), axis=1)
    used_rows = jnp.maximum(jnp.sum(members), jnp.float32(1.0))

    mine_f = silu_mix(x_all, mine_w[0], mine_w[1]).astype(jnp.bfloat16).astype(jnp.float32)
    partner_f = silu_mix(x_all, partner_in[0], partner_in[1]).astype(jnp.bfloat16).astype(jnp.float32)
    selector = members[:, None]
    energy_mine = jnp.sum(selector * mine_f * mine_f, axis=0) / used_rows
    energy_partner = jnp.sum(selector * partner_f * partner_f, axis=0) / used_rows
    cross_term = jnp.sum(selector * mine_f * partner_f, axis=0) / used_rows
    energy_low = jnp.where(is_upper, energy_partner, energy_mine)
    energy_high = jnp.where(is_upper, energy_mine, energy_partner)
    agreement = 0.5 * (1.0 + cross_term / jnp.sqrt(energy_low * energy_high + EPS))
    root_low = jnp.sqrt(energy_low + EPS)
    root_high = jnp.sqrt(energy_high + EPS)
    blend = root_low / (root_low + agreement * root_high)
    of_mine = jnp.where(is_upper, 1.0 - blend, blend)[:, None]
    of_partner = jnp.where(is_upper, blend, 1.0 - blend)[:, None]

    def merge(own, other):
        return (of_mine * own.astype(jnp.float32) + of_partner * other.astype(jnp.float32)).astype(jnp.bfloat16)

    sibling = lambda i: i ^ 1
    merged_in = merge(mine_w[:2], partner_in)
    sibling_in = along(merged_in, count, sibling)
    merged_down = merge(mine_w[2], partner_down)
    sibling_down = along(merged_down, count, sibling)

    def of_core(array):
        blocks = array.reshape(chips, CORES, rows, *array.shape[1:])
        blocks = lax.dynamic_index_in_dim(blocks, core, 1, keepdims=False)
        blocks = jnp.concatenate([blocks, blocks], axis=0)
        return lax.dynamic_slice_in_dim(blocks, chip, chips, 0).reshape(chips * rows, *array.shape[1:])

    x_core = of_core(x_all)
    own_weight = of_core(weight_of(lower_id))[:, None]
    sibling_weight = of_core(weight_of(lower_id ^ 1))[:, None]
    inner = jnp.concatenate(
        [
            (own_weight * silu_mix(x_core, merged_in[0], merged_in[1])).astype(jnp.bfloat16),
            (sibling_weight * silu_mix(x_core, sibling_in[0], sibling_in[1])).astype(jnp.bfloat16),
        ],
        axis=1,
    )
    down = jnp.concatenate([merged_down, sibling_down], axis=0)
    terms = jnp.dot(inner, down, preferred_element_type=jnp.float32).astype(jnp.bfloat16)
    terms = terms.reshape(chips, rows, -1)
    half = rows // 2
    far = chips // 2

    def add(a, b):
        return (a.astype(jnp.float32) + b.astype(jnp.float32)).astype(jnp.bfloat16)

    def collect(sign, first, second):
        at = lambda steps: terms[(sign * steps) % chips]
        far_rows = along(at(far)[first:second], count, ring(count, 2 * sign))
        near = along(at(far - 1), count, ring(count, sign))
        own = at(far - 2).astype(jnp.float32) + near.astype(jnp.float32)
        patch = own[first:second] + far_rows.astype(jnp.float32)
        parts = [patch, own[half:]] if first == 0 else [own[:half], patch]
        partial = jnp.concatenate(parts, axis=0).astype(jnp.bfloat16)
        for steps in range(far - 3, 0, -1):
            partial = add(along(partial, count, ring(count, sign)), at(steps))
        return next_layer(partial, ring(count, sign))

    onward = collect(1, 0, half)
    backward = collect(-1, half, rows)
    kept = next_layer(add(x_local, terms[0]), lambda i: i)
    handed = (kept.astype(jnp.float32) + onward.astype(jnp.float32) + backward.astype(jnp.float32)).astype(jnp.bfloat16)
    merged = jnp.concatenate([merged_in, merged_down[None]], axis=0)
    return (jnp.swapaxes(merged, 1, 2)[None, None], handed[None])


def solution(mesh):
    in_specs = (
        P("section", "expert", None),
        P("section", None, None),
        P("section", None, None),
        P("section", "expert", None, None, None),
    )
    out_specs = (P("section", "expert", None, None, None), P("section", "expert", None))
    return jax.shard_map(local, mesh=mesh, in_specs=in_specs, out_specs=out_specs, check_vma=False)
```

time: 258 us -> 185 us (0.72)
  waiting for transfers between devices: 201 us -> 71.1 us
  starting transfers between devices: 13.4 us -> 67.2 us
  local copies, waits for them, and re-layouts: 5.62 us -> 10.4 us
  matrix products: 16.7 us -> 13.8 us
    reduce_scatter x1 -> x0, waiting for transfers between devices: 64.9 us -> none  [local(): lax.psum_scatter((pair_weight[:, None] * product).astype(jnp.bfloat16), '...]
    ppermute x3 -> x13, starting transfers between devices: 13.3 us -> 67.2 us  [the longest x10 55.8 us: along(): return lax.ppermute(array, 'expert', [(i, target(i)) for i in range(count)])]
    all_gather x1, waiting for transfers between devices: 52.5 us -> 10.6 us  [local(): x_all = lax.all_gather(x_local, 'expert', axis=0, tiled=True)]
    ppermute x3 -> x13, waiting for transfers between devices: 83.2 us -> 59.8 us  [the longest x10 49.1 us: along(): return lax.ppermute(array, 'expert', [(i, target(i)) for i in range(count)])]
    another operation x0 -> x3, local copies, waits for them, and re-layouts: none -> 7.29 us
    dynamic_slice x4 -> x2, local copies, waits for them, and re-layouts: 4.88 us -> 0.02 us  [of_core(): blocks = lax.dynamic_index_in_dim(blocks, core, 1, keepdims=False)]
    dot_general x4 -> x9, matrix products: 16.7 us -> 13.8 us  [the longest x8 12.5 us: against(): lax.dot_general(activations, matrix, (((1,), (1,)), ((), ())), preferred_...]
  transfers between devices with their start and end apart: 5 -> 14, of which waited for: 5 -> 8; matrix products, arithmetic and copies ran while one was open for 3% -> 15% of each run, Pallas kernels for 0% -> 0%
where the time goes in v1:
time: 185 us; the launch traced here: 184 us
  waiting for transfers between devices  71.1 us (38%)
  starting transfers between devices  67.2 us (36%)
  between operations  15.1 us (8%)
  matrix products  13.8 us (7%)
  local copies, waits for them, and re-layouts  10.4 us (6%)
  other arithmetic  6.39 us (3%)
    ppermute x10, starting transfers between devices, along(): return lax.ppermute(array, 'expert', [(i, target(i)) for i in range(count)])  55.8 us
    ppermute x10, waiting for transfers between devices, along(): return lax.ppermute(array, 'expert', [(i, target(i)) for i in range(count)])  49.1 us
    dot_general x8, matrix products, against(): lax.dot_general(activations, matrix, (((1,), (1,)), ((), ())), preferred_...  12.5 us
    ppermute x3, starting transfers between devices, next_layer(): return lax.ppermute(array, ('section', 'expert'), route)  11.4 us
    ppermute x3, waiting for transfers between devices, next_layer(): return lax.ppermute(array, ('section', 'expert'), route)  10.8 us
    all_gather x1, waiting for transfers between devices, local(): x_all = lax.all_gather(x_local, 'expert', axis=0, tiled=True)  10.6 us
    another operation x3, local copies, waits for them, and re-layouts  7.29 us
  transfers between devices with their start and end apart: 14, of which 8 were waited for; matrix products, arithmetic and copies ran while one was open for 15% of the time, Pallas kernels for 0%

profile of v1, /device:TPU:6, one launch (start us, length us, event | category | flops | bytes accessed | tf_op | source)
XLA Modules:
  0.0 184.1 jit_solution(7417381413877710881)
XLA Ops:
  7.2 0.0 all-gather.3.cloned.1.call-start
  7.2 0.7 all-gather.3.cloned.1.call-update
  7.9 4.9 %constant_dynamic-slice_fusion.2 = (bf16[1,1,3,1024,192]{4,3,2,1,0:T(8,128)(2,1)S(1)}, bf16[1,1,3,1024,192]{4,3,2,1,0:T(8,128)(2,1)}) fusion(bf16[1,1,3,1024,384]{4,3,2,1,0:T(8,128)(2,1)} %param.7, s32[]{:T(128)S(6)} %select_n.110, s32[]{:T(128)S(6)} %select_n.111), kind=kLoop, calls=%fused_computation.90 | loop fusion | bytes 4718600 | tf_op jit(solution)/shard_map/dynamic-slice.3
  12.8 1.7 copy.6
  14.5 0.0 copy-start.1
  14.5 1.0 slice.116
  15.6 10.9 %collective-permute-start = (bf16[2,192,1024]{2,1,0:T(8,128)(2,1)}, bf16[2,192,1024]{2,1,0:T(8,128)(2,1)S(1)}, u32[]{:S(2)}, u32[]{:S(2)}) collective-permute-start(bf16[2,192,1024]{2,1,0:T(8,128)(2,1)} %slice.116), channel_id=1, source_target_pairs={{0,8},{1,9},{2,10},{3,11},{4,12},{5,13},{6,14},{7,15},{8,0},{9,1},... | collective-permute-start | bytes 2359304 | tf_op jit(solution)/shard_map/ppermute | solution.py:11
  26.5 0.0 copy-done.1
  26.5 0.7 copy.7
  27.2 1.5 select_reduce_fusion.1
  29.5 1.8 slice_bitcast_fusion.15
  31.3 35.6 %collective-permute-done = bf16[2,192,1024]{2,1,0:T(8,128)(2,1)S(1)} collective-permute-done((bf16[2,192,1024]{2,1,0:T(8,128)(2,1)}, bf16[2,192,1024]{2,1,0:T(8,128)(2,1)S(1)}, u32[]{:S(2)}, u32[]{:S(2)}) %collective-permute-start) | collective-permute-done | bytes 786464 | tf_op jit(solution)/shard_map/ppermute | solution.py:11
  66.9 9.0 %collective-permute-start.1 = (bf16[192,1024]{1,0:T(8,128)(2,1)}, bf16[192,1024]{1,0:T(8,128)(2,1)}, u32[]{:S(2)}, u32[]{:S(2)}) collective-permute-start(bf16[192,1024]{1,0:T(8,128)(2,1)} %slice_bitcast_fusion.15), channel_id=1, source_target_pairs={{0,8},{1,9},{2,10},{3,11},{4,12},{5,13},{6,14},{7,15},{8,0},{9,1},... | collective-permute-start | bytes 1179656 | tf_op jit(solution)/shard_map/ppermute | solution.py:11
  75.9 10.6 %all-gather.3.cloned.1.call-done = bf16[1,2048,1024]{2,1,0:T(8,128)(2,1)} async-done(((bf16[1,128,1024]{2,1,0:T(8,128)(2,1)}), bf16[1,2048,1024]{2,1,0:T(8,128)(2,1)}) %all-gather.3.cloned.1.call-update) | async-done | bytes 4194320 | tf_op jit(solution)/shard_map/all_gather | solution.py:60
  86.5 0.0 copy-start
  86.5 3.9 %fusion.17 = f32[2048,192]{0,1:T(8,128)S(1)} fusion(bf16[1,2048,1024]{2,1,0:T(8,128)(2,1)} %all-gather.3.cloned.1.call-done, bf16[3,192,1024]{2,1,0:T(8,128)(2,1)S(1)} %bitcast.123), kind=kOutput, calls=%fused_computation.13 | convolution fusion | flops 805306368 | bytes 6160384 | tf_op jit(solution)/shard_map/dot_general | solution.py:29
  90.3 0.0 copy-done
  90.4 1.6 fusion.29
  92.0 1.5 fusion.8
  93.5 2.1 %fusion.41 = (f32[192]{0:T(256)S(1)}, f32[192]{0:T(256)S(1)}, f32[192]{0:T(256)S(1)}) fusion(f32[2048]{0:T(1024)S(1)} %get-tuple-element.12, f32[2048,192]{0,1:T(8,128)S(1)} %fusion.29, bf16[1,2048,1024]{2,1,0:T(8,128)(2,1)S(1)} %copy-done, bf16[2,192,1024]{2,1,0:T(8,128)(2,1)S(1)} %collective-permute-done, f32[2048,192]{0,1:T(8,128)S(1)} %fusion.8), kind=kOutput, calls=%fused_computation.28 | convolution fusion | flops 811204032 | bytes 7743744 | tf_op jit(solution)/shard_map/dot_general | solution.py:29
  95.6 0.3 add_convert_fusion
  95.9 2.1 %collective-permute-start.2 = (bf16[2,192,1024]{2,1,0:T(8,128)(2,1)S(1)}, bf16[2,192,1024]{2,1,0:T(8,128)(2,1)S(1)}, u32[]{:S(2)}, u32[]{:S(2)}) collective-permute-start(bf16[2,192,1024]{2,1,0:T(8,128)(2,1)S(1)} %add_convert_fusion), channel_id=1, source_target_pairs={{0,1},{1,0},{2,3},{3,2},{4,5},{5,4},{6,7},{7,6},{8,9},{9,8},{10,11... | collective-permute-start | bytes 2359304 | tf_op jit(solution)/shard_map/ppermute | solution.py:11
  98.1 0.2 dynamic-slice_bitcast_fusion
  98.3 0.0 collective-permute-done.1
  98.3 1.2 fusion.51
  99.5 2.4 %collective-permute-start.3 = (bf16[192,1024]{1,0:T(8,128)(2,1)S(1)}, bf16[192,1024]{1,0:T(8,128)(2,1)S(1)}, u32[]{:S(2)}, u32[]{:S(2)}) collective-permute-start(bf16[192,1024]{1,0:T(8,128)(2,1)S(1)} %fusion.51), channel_id=1, source_target_pairs={{0,1},{1,0},{2,3},{3,2},{4,5},{5,4},{6,7},{7,6},{8,9},{9,8},{10,11... | collective-permute-start | bytes 1179656 | tf_op jit(solution)/shard_map/ppermute | solution.py:11
  101.9 0.8 fusion.38
  102.6 0.8 fusion.55
  103.5 0.9 fusion.43
  104.4 0.0 collective-permute-done.2
  104.4 0.8 fusion.54
  105.2 0.9 multiply_convert_fusion
  106.1 0.0 collective-permute-done.3
  106.2 1.3 convolution_convert_fusion
  107.5 5.2 %collective-permute-start.5 = (bf16[128,1024]{1,0:T(8,128)(2,1)S(1)}, bf16[128,1024]{1,0:T(8,128)(2,1)S(1)}, u32[]{:S(2)}, u32[]{:S(2)}) collective-permute-start(bf16[128,1024]{1,0:T(8,128)(2,1)S(1)} %get-tuple-element.24), channel_id=1, source_target_pairs={{0,2},{1,3},{2,4},{3,5},{4,6},{5,7},{6,8},{7,9},{8,10},{9,11},{10,... | collective-permute-start | bytes 786440 | tf_op jit(solution)/shard_map/ppermute | solution.py:11
  112.7 1.9 %collective-permute-start.9 = (bf16[128,1024]{1,0:T(8,128)(2,1)S(1)}, bf16[128,1024]{1,0:T(8,128)(2,1)S(1)}, u32[]{:S(2)}, u32[]{:S(2)}) collective-permute-start(bf16[128,1024]{1,0:T(8,128)(2,1)S(1)} %get-tuple-element.25), channel_id=1, source_target_pairs={{0,14},{1,15},{2,0},{3,1},{4,2},{5,3},{6,4},{7,5},{8,6},{9,7},{10,... | collective-permute-start | bytes 786440 | tf_op jit(solution)/shard_map/ppermute | solution.py:11
  114.7 5.5 %collective-permute-start.10 = (bf16[64,1024]{1,0:T(8,128)(2,1)S(1)}, bf16[64,1024]{1,0:T(8,128)(2,1)S(1)}, u32[]{:S(2)}, u32[]{:S(2)}) collective-permute-start(bf16[64,1024]{1,0:T(8,128)(2,1)S(1)} %get-tuple-element.21), channel_id=1, source_target_pairs={{0,12},{1,13},{2,14},{3,15},{4,0},{5,1},{6,2},{7,3},{8,4},{9,5},{1... | collective-permute-start | bytes 393224 | tf_op jit(solution)/shard_map/ppermute | solution.py:11
  120.2 12.9 %collective-permute-start.6 = (bf16[64,1024]{1,0:T(8,128)(2,1)S(1)}, bf16[64,1024]{1,0:T(8,128)(2,1)S(1)}, u32[]{:S(2)}, u32[]{:S(2)}) collective-permute-start(bf16[64,1024]{1,0:T(8,128)(2,1)S(1)} %get-tuple-element.20), channel_id=1, source_target_pairs={{0,4},{1,5},{2,6},{3,7},{4,8},{5,9},{6,10},{7,11},{8,12},{9,13},{1... | collective-permute-start | bytes 393224 | tf_op jit(solution)/shard_map/ppermute | solution.py:11
  133.0 0.0 collective-permute-done.5
  133.1 0.0 collective-permute-done.9
  133.1 0.2 convert_add_fusion.2
  133.2 0.0 copy-start.2
  133.3 7.9 %collective-permute-done.10 = bf16[64,1024]{1,0:T(8,128)(2,1)S(1)} collective-permute-done((bf16[64,1024]{1,0:T(8,128)(2,1)S(1)}, bf16[64,1024]{1,0:T(8,128)(2,1)S(1)}, u32[]{:S(2)}, u32[]{:S(2)}) %collective-permute-start.10) | collective-permute-done | bytes 131104 | tf_op jit(solution)/shard_map/ppermute | solution.py:11
  141.3 1.9 %collective-permute-start.11 = (bf16[128,1024]{1,0:T(8,128)(2,1)S(1)}, bf16[128,1024]{1,0:T(8,128)(2,1)S(1)}, u32[]{:S(2)}, u32[]{:S(2)}) collective-permute-start(bf16[128,1024]{1,0:T(8,128)(2,1)S(1)} %pad_maximum_fusion.1), channel_id=1, source_target_pairs={{0,14},{1,15},{2,0},{3,1},{4,2},{5,3},{6,4},{7,5},{8,6},{9,7},{10,... | collective-permute-start | bytes 786440 | tf_op jit(solution)/shard_map/ppermute | solution.py:11
  143.2 0.0 collective-permute-done.6
  143.3 3.9 %collective-permute-start.7 = (bf16[128,1024]{1,0:T(8,128)(2,1)S(1)}, bf16[128,1024]{1,0:T(8,128)(2,1)S(1)}, u32[]{:S(2)}, u32[]{:S(2)}) collective-permute-start(bf16[128,1024]{1,0:T(8,128)(2,1)S(1)} %pad_maximum_fusion), channel_id=1, source_target_pairs={{0,2},{1,3},{2,4},{3,5},{4,6},{5,7},{6,8},{7,9},{8,10},{9,11},{10,... | collective-permute-start | bytes 786440 | tf_op jit(solution)/shard_map/ppermute | solution.py:11
  147.2 2.3 %collective-permute-done.11 = bf16[128,1024]{1,0:T(8,128)(2,1)S(1)} collective-permute-done((bf16[128,1024]{1,0:T(8,128)(2,1)S(1)}, bf16[128,1024]{1,0:T(8,128)(2,1)S(1)}, u32[]{:S(2)}, u32[]{:S(2)}) %collective-permute-start.11) | collective-permute-done | bytes 262176 | tf_op jit(solution)/shard_map/ppermute | solution.py:11
  149.5 3.2 %collective-permute-done.7 = bf16[128,1024]{1,0:T(8,128)(2,1)S(1)} collective-permute-done((bf16[128,1024]{1,0:T(8,128)(2,1)S(1)}, bf16[128,1024]{1,0:T(8,128)(2,1)S(1)}, u32[]{:S(2)}, u32[]{:S(2)}) %collective-permute-start.7) | collective-permute-done | bytes 262176 | tf_op jit(solution)/shard_map/ppermute | solution.py:11
  152.8 0.0 copy-done.2
  152.8 0.3 fusion.52
  153.1 2.9 %collective-permute-start.12 = (bf16[128,1024]{1,0:T(8,128)(2,1)S(1)}, bf16[128,1024]{1,0:T(8,128)(2,1)S(1)}, u32[]{:S(2)}, u32[]{:S(2)}) collective-permute-start(bf16[128,1024]{1,0:T(8,128)(2,1)S(1)} %get-tuple-element.18), channel_id=1, source_target_pairs={{0,30},{1,31},{2,16},{3,17},{4,18},{5,19},{6,20},{7,21},{8,22},{9,... | collective-permute-start | bytes 786440 | tf_op jit(solution)/shard_map/ppermute | solution.py:25
  156.0 5.0 %collective-permute-start.8 = (bf16[128,1024]{1,0:T(8,128)(2,1)S(1)}, bf16[128,1024]{1,0:T(8,128)(2,1)S(1)}, u32[]{:S(2)}, u32[]{:S(2)}) collective-permute-start(bf16[128,1024]{1,0:T(8,128)(2,1)S(1)} %get-tuple-element.19), channel_id=1, source_target_pairs={{0,18},{1,19},{2,20},{3,21},{4,22},{5,23},{6,24},{7,25},{8,26},{9,... | collective-permute-start | bytes 786440 | tf_op jit(solution)/shard_map/ppermute | solution.py:25
  161.0 3.5 %collective-permute-start.4 = (bf16[128,1024]{1,0:T(8,128)(2,1)S(1)}, bf16[128,1024]{1,0:T(8,128)(2,1)S(1)}, u32[]{:S(2)}, u32[]{:S(2)}) collective-permute-start(bf16[128,1024]{1,0:T(8,128)(2,1)S(1)} %get-tuple-element.17), channel_id=1, source_target_pairs={{0,16},{1,17},{2,18},{3,19},{4,20},{5,21},{6,22},{7,23},{8,24},{9,... | collective-permute-start | bytes 786440 | tf_op jit(solution)/shard_map/ppermute | solution.py:25
  164.5 1.1 maximum_bitcast_fusion
  165.6 0.7 collective-permute-done.12
  166.4 8.4 %collective-permute-done.8 = bf16[128,1024]{1,0:T(8,128)(2,1)S(1)} collective-permute-done((bf16[128,1024]{1,0:T(8,128)(2,1)S(1)}, bf16[128,1024]{1,0:T(8,128)(2,1)S(1)}, u32[]{:S(2)}, u32[]{:S(2)}) %collective-permute-start.8) | collective-permute-done | bytes 262176 | tf_op jit(solution)/shard_map/ppermute | solution.py:25
  174.8 1.6 collective-permute-done.4
  176.4 0.8 fusion.60
  (13 shorter events, 0.2 us)
Async XLA Ops:
  7.2 79.3 %all-gather.3.cloned.1.call-start = ((), (), s32[]{:S(2)}) async-start(), calls=%async_computation | async-start | bytes 4456448 | tf_op jit(solution)/shard_map/all_gather | solution.py:60
  14.5 12.0 %copy-start.1 = (bf16[1,1,3,1024,192]{3,4,2,1,0:T(8,128)(2,1)}, bf16[1,1,3,1024,192]{3,4,2,1,0:T(8,128)(2,1)S(1)}, u32[]{:S(2)}) copy-start(bf16[1,1,3,1024,192]{3,4,2,1,0:T(8,128)(2,1)S(1)} %copy.6) | copy-start | bytes 3538948
  15.6 51.3 %collective-permute-start = (bf16[2,192,1024]{2,1,0:T(8,128)(2,1)}, bf16[2,192,1024]{2,1,0:T(8,128)(2,1)S(1)}, u32[]{:S(2)}, u32[]{:S(2)}) collective-permute-start(bf16[2,192,1024]{2,1,0:T(8,128)(2,1)} %slice.116), channel_id=1, source_target_pairs={{0,8},{1,9},{2,10},{3,11},{4,12},{5,13},{6,14},{7,15},{8,0},{9,1},... | collective-permute-start | bytes 2359304 | tf_op jit(solution)/shard_map/ppermute | solution.py:11
  66.9 31.4 %collective-permute-start.1 = (bf16[192,1024]{1,0:T(8,128)(2,1)}, bf16[192,1024]{1,0:T(8,128)(2,1)}, u32[]{:S(2)}, u32[]{:S(2)}) collective-permute-start(bf16[192,1024]{1,0:T(8,128)(2,1)} %slice_bitcast_fusion.15), channel_id=1, source_target_pairs={{0,8},{1,9},{2,10},{3,11},{4,12},{5,13},{6,14},{7,15},{8,0},{9,1},... | collective-permute-start | bytes 1179656 | tf_op jit(solution)/shard_map/ppermute | solution.py:11
  86.5 3.9 %copy-start = (bf16[1,2048,1024]{2,1,0:T(8,128)(2,1)S(1)}, bf16[1,2048,1024]{2,1,0:T(8,128)(2,1)}, u32[]{:S(2)}) copy-start(bf16[1,2048,1024]{2,1,0:T(8,128)(2,1)} %all-gather.3.cloned.1.call-done) | copy-start | bytes 12582916
  95.9 8.5 %collective-permute-start.2 = (bf16[2,192,1024]{2,1,0:T(8,128)(2,1)S(1)}, bf16[2,192,1024]{2,1,0:T(8,128)(2,1)S(1)}, u32[]{:S(2)}, u32[]{:S(2)}) collective-permute-start(bf16[2,192,1024]{2,1,0:T(8,128)(2,1)S(1)} %add_convert_fusion), channel_id=1, source_target_pairs={{0,1},{1,0},{2,3},{3,2},{4,5},{5,4},{6,7},{7,6},{8,9},{9,8},{10,11... | collective-permute-start | bytes 2359304 | tf_op jit(solution)/shard_map/ppermute | solution.py:11
  99.5 6.7 %collective-permute-start.3 = (bf16[192,1024]{1,0:T(8,128)(2,1)S(1)}, bf16[192,1024]{1,0:T(8,128)(2,1)S(1)}, u32[]{:S(2)}, u32[]{:S(2)}) collective-permute-start(bf16[192,1024]{1,0:T(8,128)(2,1)S(1)} %fusion.51), channel_id=1, source_target_pairs={{0,1},{1,0},{2,3},{3,2},{4,5},{5,4},{6,7},{7,6},{8,9},{9,8},{10,11... | collective-permute-start | bytes 1179656 | tf_op jit(solution)/shard_map/ppermute | solution.py:11
  107.5 25.5 %collective-permute-start.5 = (bf16[128,1024]{1,0:T(8,128)(2,1)S(1)}, bf16[128,1024]{1,0:T(8,128)(2,1)S(1)}, u32[]{:S(2)}, u32[]{:S(2)}) collective-permute-start(bf16[128,1024]{1,0:T(8,128)(2,1)S(1)} %get-tuple-element.24), channel_id=1, source_target_pairs={{0,2},{1,3},{2,4},{3,5},{4,6},{5,7},{6,8},{7,9},{8,10},{9,11},{10,... | collective-permute-start | bytes 786440 | tf_op jit(solution)/shard_map/ppermute | solution.py:11
  112.7 20.3 %collective-permute-start.9 = (bf16[128,1024]{1,0:T(8,128)(2,1)S(1)}, bf16[128,1024]{1,0:T(8,128)(2,1)S(1)}, u32[]{:S(2)}, u32[]{:S(2)}) collective-permute-start(bf16[128,1024]{1,0:T(8,128)(2,1)S(1)} %get-tuple-element.25), channel_id=1, source_target_pairs={{0,14},{1,15},{2,0},{3,1},{4,2},{5,3},{6,4},{7,5},{8,6},{9,7},{10,... | collective-permute-start | bytes 786440 | tf_op jit(solution)/shard_map/ppermute | solution.py:11
  114.7 26.5 %collective-permute-start.10 = (bf16[64,1024]{1,0:T(8,128)(2,1)S(1)}, bf16[64,1024]{1,0:T(8,128)(2,1)S(1)}, u32[]{:S(2)}, u32[]{:S(2)}) collective-permute-start(bf16[64,1024]{1,0:T(8,128)(2,1)S(1)} %get-tuple-element.21), channel_id=1, source_target_pairs={{0,12},{1,13},{2,14},{3,15},{4,0},{5,1},{6,2},{7,3},{8,4},{9,5},{1... | collective-permute-start | bytes 393224 | tf_op jit(solution)/shard_map/ppermute | solution.py:11
  120.2 23.1 %collective-permute-start.6 = (bf16[64,1024]{1,0:T(8,128)(2,1)S(1)}, bf16[64,1024]{1,0:T(8,128)(2,1)S(1)}, u32[]{:S(2)}, u32[]{:S(2)}) collective-permute-start(bf16[64,1024]{1,0:T(8,128)(2,1)S(1)} %get-tuple-element.20), channel_id=1, source_target_pairs={{0,4},{1,5},{2,6},{3,7},{4,8},{5,9},{6,10},{7,11},{8,12},{9,13},{1... | collective-permute-start | bytes 393224 | tf_op jit(solution)/shard_map/ppermute | solution.py:11
  133.2 19.5 %copy-start.2 = (bf16[1,128,1024]{2,1,0:T(8,128)(2,1)S(1)}, bf16[1,128,1024]{2,1,0:T(8,128)(2,1)}, u32[]{:S(2)}) copy-start(bf16[1,128,1024]{2,1,0:T(8,128)(2,1)} %param.4) | copy-start | bytes 786436
  141.3 8.3 %collective-permute-start.11 = (bf16[128,1024]{1,0:T(8,128)(2,1)S(1)}, bf16[128,1024]{1,0:T(8,128)(2,1)S(1)}, u32[]{:S(2)}, u32[]{:S(2)}) collective-permute-start(bf16[128,1024]{1,0:T(8,128)(2,1)S(1)} %pad_maximum_fusion.1), channel_id=1, source_target_pairs={{0,14},{1,15},{2,0},{3,1},{4,2},{5,3},{6,4},{7,5},{8,6},{9,7},{10,... | collective-permute-start | bytes 786440 | tf_op jit(solution)/shard_map/ppermute | solution.py:11
  143.3 9.5 %collective-permute-start.7 = (bf16[128,1024]{1,0:T(8,128)(2,1)S(1)}, bf16[128,1024]{1,0:T(8,128)(2,1)S(1)}, u32[]{:S(2)}, u32[]{:S(2)}) collective-permute-start(bf16[128,1024]{1,0:T(8,128)(2,1)S(1)} %pad_maximum_fusion), channel_id=1, source_target_pairs={{0,2},{1,3},{2,4},{3,5},{4,6},{5,7},{6,8},{7,9},{8,10},{9,11},{10,... | collective-permute-start | bytes 786440 | tf_op jit(solution)/shard_map/ppermute | solution.py:11
  153.1 13.3 %collective-permute-start.12 = (bf16[128,1024]{1,0:T(8,128)(2,1)S(1)}, bf16[128,1024]{1,0:T(8,128)(2,1)S(1)}, u32[]{:S(2)}, u32[]{:S(2)}) collective-permute-start(bf16[128,1024]{1,0:T(8,128)(2,1)S(1)} %get-tuple-element.18), channel_id=1, source_target_pairs={{0,30},{1,31},{2,16},{3,17},{4,18},{5,19},{6,20},{7,21},{8,22},{9,... | collective-permute-start | bytes 786440 | tf_op jit(solution)/shard_map/ppermute | solution.py:25
  156.0 18.8 %collective-permute-start.8 = (bf16[128,1024]{1,0:T(8,128)(2,1)S(1)}, bf16[128,1024]{1,0:T(8,128)(2,1)S(1)}, u32[]{:S(2)}, u32[]{:S(2)}) collective-permute-start(bf16[128,1024]{1,0:T(8,128)(2,1)S(1)} %get-tuple-element.19), channel_id=1, source_target_pairs={{0,18},{1,19},{2,20},{3,21},{4,22},{5,23},{6,24},{7,25},{8,26},{9,... | collective-permute-start | bytes 786440 | tf_op jit(solution)/shard_map/ppermute | solution.py:25
  161.0 15.4 %collective-permute-start.4 = (bf16[128,1024]{1,0:T(8,128)(2,1)S(1)}, bf16[128,1024]{1,0:T(8,128)(2,1)S(1)}, u32[]{:S(2)}, u32[]{:S(2)}) collective-permute-start(bf16[128,1024]{1,0:T(8,128)(2,1)S(1)} %get-tuple-element.17), channel_id=1, source_target_pairs={{0,16},{1,17},{2,18},{3,19},{4,20},{5,21},{6,22},{7,23},{8,24},{9,... | collective-permute-start | bytes 786440 | tf_op jit(solution)/shard_map/ppermute | solution.py:25
Sparse Core Ops, SparseCore 0:
  10.1 76.3 all-gather.2

commit v2 on v1

v2 whole, which is shorter than its diff:
```python
import jax
import jax.numpy as jnp
from jax import lax
from jax.experimental import pallas as pl
from jax.experimental.pallas import tpu as pltpu
from jax.sharding import PartitionSpec as P

EPS = 1e-06
CORES = 2
SLAB = 256


def along(array, count, target):
    return lax.ppermute(array, "expert", [(i, target(i)) for i in range(count)])


def ring(count, steps):
    return lambda i: (i + CORES * steps) % count


def next_layer(array, target):
    layers, count = lax.axis_size("section"), lax.axis_size("expert")
    route = [
        (layer * count + i, (layer + 1) * count + target(i))
        for layer in range(layers - 1)
        for i in range(count)
    ]
    return lax.ppermute(array, ("section", "expert"), route)


def against(matrix, activations):
    return lax.dot_general(
        matrix, activations, (((1,), (1,)), ((), ())), preferred_element_type=jnp.float32
    )


def silu_mix(gate, up):
    return gate / (1.0 + jnp.exp(-gate)) * up


def merge(is_upper, blend, own, other):
    of_own = jnp.where(is_upper, 1.0 - blend, blend)
    of_other = jnp.where(is_upper, blend, 1.0 - blend)
    return (of_own * own.astype(jnp.float32) + of_other * other.astype(jnp.float32)).astype(jnp.bfloat16)


def split_kernel(upper, projection, kept_in, kept_down, sent_in, sent_down):
    units = kept_down.shape[0]
    part = pl.program_id(0)
    turned = projection[0].T

    def put(kept, sent, at):
        @pl.when(upper[0] == 1)
        def _():
            kept[at, :] = turned[units:]
            sent[at, :] = turned[:units]

        @pl.when(upper[0] == 0)
        def _():
            kept[at, :] = turned[:units]
            sent[at, :] = turned[units:]

    for matrix in range(2):

        @pl.when(part == matrix)
        def _(matrix=matrix):
            put(kept_in, sent_in, pl.ds(matrix * units, units))

    @pl.when(part == 2)
    def _():
        put(kept_down, sent_down, pl.ds(0, units))


def blend_kernel(upper, members, x, own, other, merged, blend_out, sums, count):
    step = pl.program_id(0)
    units = sums.shape[1]
    lanes = sums.shape[2]

    @pl.when(step == 0)
    def _():
        sums[...] = jnp.zeros_like(sums)
        count[...] = jnp.zeros_like(count)

    def fold(array):
        return sum(array[:, i : i + lanes] for i in range(0, array.shape[1], lanes))

    for start in range(0, x.shape[0], SLAB):
        slab = pl.ds(start, SLAB)
        chosen = members[0][:, start : start + SLAB]
        hidden = []
        for weights in (own, other):
            out = against(weights[...], x[slab, :])
            hidden.append(silu_mix(out[:units], out[units:]).astype(jnp.bfloat16).astype(jnp.float32))
        mine, theirs = hidden
        weighted = chosen * mine
        sums[0] += fold(weighted * mine)
        sums[1] += fold(chosen * theirs * theirs)
        sums[2] += fold(weighted * theirs)
        count[...] += fold(chosen)

    @pl.when(step == pl.num_programs(0) - 1)
    def _():
        is_upper = upper[0] == 1
        used = jnp.maximum(jnp.sum(count[...], axis=1, keepdims=True), 1.0)
        energy_own, energy_other, cross_term = (
            jnp.sum(sums[i], axis=1, keepdims=True) / used for i in range(3)
        )
        energy_low = jnp.where(is_upper, energy_other, energy_own)
        energy_high = jnp.where(is_upper, energy_own, energy_other)
        agreement = 0.5 * (1.0 + cross_term / jnp.sqrt(energy_low * energy_high + EPS))
        root_low = jnp.sqrt(energy_low + EPS)
        root_high = jnp.sqrt(energy_high + EPS)
        blend = root_low / (root_low + agreement * root_high)
        blend_out[...] = jnp.broadcast_to(blend, blend_out.shape)
        for part in range(2):
            at = pl.ds(part * units, units)
            merged[at, :] = merge(is_upper, blend, own[at, :], other[at, :])


def weighted_terms(gate, up, down, x, weights, outs):
    units = gate.shape[0] // 2
    hidden = jnp.concatenate([ref[...] for ref in x], axis=0)
    hidden = silu_mix(against(gate[...], hidden), against(up[...], hidden))
    weight = jnp.concatenate([ref[0] for ref in weights], axis=1)
    inner = jnp.concatenate([hidden[:units] * weight[:1], hidden[units:] * weight[1:]], axis=0)
    out = lax.dot_general(
        inner.astype(jnp.bfloat16), down[...], (((0,), (0,)), ((), ())), preferred_element_type=jnp.float32
    ).astype(jnp.bfloat16)
    start = 0
    for ref in outs:
        ref[...] = out[start : start + ref.shape[0]]
        start += ref.shape[0]


def first_kernel(
    places, upper, weight_a, weight_b, weight_c, weight_d, x_a, x_b, x_c, x_d, merged_in, own_down, other_down,
    next_own, next_other, next_own_down, next_down, blend, next_blend, term_a, term_b, term_c, term_d, term_e, gate, up, down
):
    units = blend.shape[0]
    is_upper = upper[0] == 1
    mine = blend[:, :1]
    theirs = next_blend[:, :1]
    gate[:units] = merged_in[:units]
    up[:units] = merged_in[units:]
    down[:units] = merge(is_upper, mine, own_down[...], other_down[...])
    gate[units:] = merge(is_upper, theirs, next_own[:units], next_other[:units])
    up[units:] = merge(is_upper, theirs, next_own[units:], next_other[units:])
    down[units:] = merge(is_upper, theirs, next_own_down[...], next_down[...])
    weighted_terms(gate, up, down, (x_a, x_b), (weight_a, weight_b), (term_a, term_b, term_c))
    weighted_terms(gate, up, down, (x_c, x_d), (weight_c, weight_d), (term_d, term_e))


def terms_kernel(places, weight_a, weight_b, x_a, x_b, gate, up, down, *outs):
    for step in range(len(outs) // 2):

        @pl.when(pl.program_id(0) == step)
        def _(step=step):
            weighted_terms(gate, up, down, (x_a, x_b), (weight_a, weight_b), outs[2 * step : 2 * step + 2])


def local(tokens, routes, route_weight, projections):
    x_local = tokens[0]
    layer_routes = routes[0]
    layer_weight = route_weight[0]
    count = lax.axis_size("expert")
    pair_count = count // 2
    chips = count // CORES
    me = lax.axis_index("expert")
    chip, core = me // CORES, me % CORES
    is_upper = me >= pair_count
    upper = is_upper.astype(jnp.int32)[None]
    matrices, features, full_units = projections.shape[2:]
    units = full_units // 2
    rows = x_local.shape[0]
    across = lambda i: (i + pair_count) % count
    sibling = lambda i: i ^ 1

    x_all = lax.all_gather(x_local, "expert", axis=0, tiled=True)
    half_spec = lambda parts: pl.BlockSpec((parts * units, features), lambda i, *_: (0, 0))
    half = lambda parts: jax.ShapeDtypeStruct((parts * units, features), jnp.bfloat16)
    mine_in, mine_down, send_in, send_down = pl.pallas_call(
        split_kernel,
        grid_spec=pltpu.PrefetchScalarGridSpec(
            num_scalar_prefetch=1,
            grid=(matrices,),
            in_specs=[pl.BlockSpec((1, features, full_units), lambda i, *_: (i, 0, 0))],
            out_specs=[half_spec(2), half_spec(1), half_spec(2), half_spec(1)],
        ),
        out_shape=[half(2), half(1), half(2), half(1)],
        compiler_params=pltpu.CompilerParams(vmem_limit_bytes=32 << 20),
        cost_estimate=pl.CostEstimate(flops=0, bytes_accessed=4 * matrices * features * full_units, transcendentals=0),
        name="split",
    )(upper, projections[0, 0])
    partner_in = along(send_in, count, across)
    send_down, partner_in = lax.optimization_barrier((send_down, partner_in))
    partner_down = along(send_down, count, across)
    next_other = along(partner_in, count, sibling)

    members, row_weight = [], []
    for pair in (me % pair_count, (me % pair_count) ^ 1):
        named = (layer_routes == pair) | (layer_routes == pair + pair_count)
        members.append(jnp.sum(named.astype(jnp.float32), axis=1))
        row_weight.append(jnp.sum(jnp.where(named, layer_weight, jnp.float32(0.0)), axis=1))
    row_weight = jnp.stack([array.reshape(count, rows) for array in row_weight], axis=1)
    far = chips // 2
    order = [far, far - 1, far + 1, 0, *(s for k in range(far - 2, 0, -1) for s in (k, chips - k))]
    places = ((chip + jnp.array(order, jnp.int32)) % chips) * CORES + core
    member, row_weight, first_places, places, kept_in, kept_down = lax.optimization_barrier(
        (members[0].reshape(-1, 1, 4 * rows), row_weight, places[:4], places[4:], mine_in, mine_down)
    )
    next_own = along(kept_in, count, sibling)
    next_own_down = along(kept_down, count, sibling)

    whole = lambda shape: pl.BlockSpec(shape, lambda i, *_: (0,) * len(shape))
    held = pl.BlockSpec(memory_space=pltpu.VMEM)
    total = x_all.shape[0]
    group = 4 * rows
    merged_in, blend = pl.pallas_call(
        blend_kernel,
        grid_spec=pltpu.PrefetchScalarGridSpec(
            num_scalar_prefetch=1,
            grid=(total // group,),
            in_specs=[
                pl.BlockSpec((1, 1, group), lambda i, *_: (i, 0, 0)),
                pl.BlockSpec((group, features), lambda i, *_: (i, 0)),
                held,
                held,
            ],
            out_specs=[whole((2 * units, features)), whole((units, 128))],
            scratch_shapes=[pltpu.VMEM((3, units, 128), jnp.float32), pltpu.VMEM((1, 128), jnp.float32)],
        ),
        out_shape=[
            jax.ShapeDtypeStruct((2 * units, features), jnp.bfloat16),
            jax.ShapeDtypeStruct((units, 128), jnp.float32),
        ],
        compiler_params=pltpu.CompilerParams(vmem_limit_bytes=32 << 20),
        cost_estimate=pl.CostEstimate(flops=8 * total * units * features, bytes_accessed=2 * total * features, transcendentals=0),
        name="blend",
    )(upper, member, x_all, mine_in, partner_in)
    next_blend = along(blend, count, sibling)
    partner_down, blend = lax.optimization_barrier((partner_down, blend))
    next_down = along(partner_down, count, sibling)

    weight_spec = lambda k: pl.BlockSpec((1, CORES, rows), lambda i, place, *_: (place[2 * i + k], 0, 0))
    x_spec = lambda k: pl.BlockSpec((rows, features), lambda i, place, *_: (place[2 * i + k], 0))
    blocks_in = lambda number: [weight_spec(k) for k in range(number)] + [x_spec(k) for k in range(number)]
    both = (2 * units, features)
    block = jax.ShapeDtypeStruct((rows, features), jnp.bfloat16)
    part = jax.ShapeDtypeStruct((rows // 2, features), jnp.bfloat16)
    low_rows, high_rows, *firsts, gate, up, down = pl.pallas_call(
        first_kernel,
        grid_spec=pltpu.PrefetchScalarGridSpec(
            num_scalar_prefetch=2,
            grid=(1,),
            in_specs=[
                *blocks_in(4),
                *[held] * 9,
            ],
            out_specs=[whole(part.shape)] * 2 + [whole(block.shape)] * 3 + [whole(both)] * 3,
        ),
        out_shape=[part] * 2 + [block] * 3 + [jax.ShapeDtypeStruct(both, jnp.bfloat16)] * 3,
        compiler_params=pltpu.CompilerParams(vmem_limit_bytes=40 << 20),
        cost_estimate=pl.CostEstimate(flops=24 * rows * units * features, bytes_accessed=20 * units * features, transcendentals=0),
        name="first",
    )(first_places, upper, *[row_weight] * 4, *[x_all] * 4, merged_in, mine_down, partner_down,
      next_own, next_other, next_own_down, next_down, blend, next_blend)
    others = pl.pallas_call(
        terms_kernel,
        grid_spec=pltpu.PrefetchScalarGridSpec(
            num_scalar_prefetch=1,
            grid=(chips // 2 - 2,),
            in_specs=[*blocks_in(2), whole(both), whole(both), whole(both)],
            out_specs=[whole(block.shape)] * (chips - 4),
        ),
        out_shape=[block] * (chips - 4),
        compiler_params=pltpu.CompilerParams(vmem_limit_bytes=40 << 20),
        cost_estimate=pl.CostEstimate(flops=24 * rows * units * features, bytes_accessed=4 * chips * rows * features, transcendentals=0),
        name="terms",
    )(places, row_weight, row_weight, x_all, x_all, gate, up, down)
    terms = dict(zip(order[1:], [*firsts, *others]))

    def add(*parts):
        return sum(part.astype(jnp.float32) for part in parts).astype(jnp.bfloat16)

    half = rows // 2
    behind, ahead = along(low_rows, count, ring(count, 1)), along(high_rows, count, ring(count, -1))
    three, minus_three = terms[far - 1], terms[chips - far + 1]
    grown = jnp.concatenate([add(behind, three[:half]), three[half:]], axis=0)
    minus_grown = jnp.concatenate([minus_three[:half], add(ahead, minus_three[half:])], axis=0)
    grown, minus_grown, one, minus_one = lax.optimization_barrier((grown, minus_grown, terms[1], terms[chips - 1]))
    grown = add(along(grown, count, ring(count, 1)), terms[far - 2])
    minus_grown = add(along(minus_grown, count, ring(count, -1)), terms[chips - far + 2])
    here = add(x_local, terms[0], along(one, count, ring(count, 1)), along(minus_one, count, ring(count, -1)))
    handed = add(
        next_layer(grown, ring(count, far - 2)),
        next_layer(minus_grown, ring(count, 2 - far)),
        next_layer(here, lambda i: i),
    )
    own = jnp.stack([gate[:units], up[:units], down[:units]])
    return (jnp.swapaxes(own, 1, 2)[None, None], handed[None])


def solution(mesh):
    in_specs = (
        P("section", "expert", None),
        P("section", None, None),
        P("section", None, None),
        P("section", "expert", None, None, None),
    )
    out_specs = (P("section", "expert", None, None, None), P("section", "expert", None))
    return jax.shard_map(local, mesh=mesh, in_specs=in_specs, out_specs=out_specs, check_vma=False)
```

time: 185 us -> 172 us (0.930)
  Pallas kernels: 0 us -> 14.1 us
  matrix products: 13.8 us -> 0 us
  local copies, waits for them, and re-layouts: 10.4 us -> 4.04 us
  other arithmetic: 6.39 us -> 2.48 us
    pallas_call x0 -> x4, Pallas kernels: none -> 14.1 us  [the longest x1 6.91 us: local(): pl.pallas_call(blend_kernel, grid_spec=pltpu.PrefetchScalarGridSpec(num_s...]
    dot_general x9 -> x0, matrix products: 13.8 us -> none  [the longest x8 12.5 us: against(): lax.dot_general(activations, matrix, (((1,), (1,)), ((), ())), preferred_...]
    ppermute x10 -> x13, waiting for transfers between devices: 49.1 us -> 40.6 us  [along(): return lax.ppermute(array, 'expert', [(i, target(i)) for i in range(count)])]
    another operation x3 -> x2, local copies, waits for them, and re-layouts: 7.29 us -> 0.08 us  [local(): own = jnp.stack([gate[:units], up[:units], down[:units]])]
    all_gather x1, waiting for transfers between devices: 10.6 us -> 16.2 us  [local(): x_all = lax.all_gather(x_local, 'expert', axis=0, tiled=True)]
    unnamed x6 -> x14, local copies, waits for them, and re-layouts: 0.02 us -> 3.87 us
    ppermute x10 -> x13, starting transfers between devices: 55.8 us -> 52.4 us  [along(): return lax.ppermute(array, 'expert', [(i, target(i)) for i in range(count)])]
    ppermute x3, waiting for transfers between devices: 10.8 us -> 13.3 us  [next_layer(): return lax.ppermute(array, ('section', 'expert'), route)]
  transfers between devices with their start and end apart: 14 -> 17, of which waited for: 8 -> 7; matrix products, arithmetic and copies ran while one was open for 15% -> 1% of each run, Pallas kernels for 0% -> 7%
where the time goes in v2:
time: 172 us
  waiting for transfers between devices  70.7 us (41%)
  starting transfers between devices  66 us (38%)
  between operations  14.4 us (8%)
  Pallas kernels  14.1 us (8%)
  local copies, waits for them, and re-layouts  4.04 us (2%)
  other arithmetic  2.48 us (1%)
    ppermute x13, starting transfers between devices, along(): return lax.ppermute(array, 'expert', [(i, target(i)) for i in range(count)])  52.4 us
    ppermute x13, waiting for transfers between devices, along(): return lax.ppermute(array, 'expert', [(i, target(i)) for i in range(count)])  40.6 us
    all_gather x1, waiting for transfers between devices, local(): x_all = lax.all_gather(x_local, 'expert', axis=0, tiled=True)  16.2 us
    ppermute x3, starting transfers between devices, next_layer(): return lax.ppermute(array, ('section', 'expert'), route)  13.6 us
    ppermute x3, waiting for transfers between devices, next_layer(): return lax.ppermute(array, ('section', 'expert'), route)  13.3 us
    pallas_call x1, Pallas kernels, local(): pl.pallas_call(blend_kernel, grid_spec=pltpu.PrefetchScalarGridSpec(num_s...  6.91 us
    unnamed x14, local copies, waits for them, and re-layouts  3.87 us
  transfers between devices with their start and end apart: 17, of which 7 were waited for; matrix products, arithmetic and copies ran while one was open for 1% of the time, Pallas kernels for 7%

profile of v2, /device:TPU:6, one launch (start us, length us, event | category | flops | bytes accessed | tf_op | source)
XLA Modules:
  0.0 171.9 jit_solution(7546759947379917185)
XLA Ops:
  7.2 0.0 all-gather.3.cloned.1.call-start
  7.2 0.7 all-gather.3.cloned.1.call-update
  7.9 0.0 copy-start.2
  7.9 1.7 copy-done.2
  9.6 0.0 copy-start.4
  9.6 0.0 copy-start.5
  9.6 0.0 copy-start.6
  9.6 1.9 %split.1 = (bf16[384,1024]{1,0:T(8,128)(2,1)}, bf16[192,1024]{1,0:T(8,128)(2,1)S(1)}, bf16[384,1024]{1,0:T(8,128)(2,1)S(1)}, bf16[192,1024]{1,0:T(8,128)(2,1)S(1)}) custom-call(s32[1]{0:T(128)} %bitcast.3.upper, bf16[3,1024,384]{2,1,0:T(8,128)(2,1)S(1)} %bitcast.28), custom_call_target="tpu_custom_call" | custom-call | bytes 4718592 | tf_op jit(solution)/shard_map/split/pallas_call | solution.py:181
  11.4 10.9 %collective-permute-start = (bf16[384,1024]{1,0:T(8,128)(2,1)S(1)}, bf16[384,1024]{1,0:T(8,128)(2,1)}, u32[]{:S(2)}, u32[]{:S(2)}) collective-permute-start(bf16[384,1024]{1,0:T(8,128)(2,1)S(1)} %get-tuple-element.40), channel_id=1, source_target_pairs={{0,8},{1,9},{2,10},{3,11},{4,12},{5,13},{6,14},{7,15},{8,0},{9,1},... | collective-permute-start | bytes 2359304 | tf_op jit(solution)/shard_map/ppermute | solution.py:14
  22.4 0.0 copy-done.4
  22.4 0.0 copy-done.5
  22.4 0.1 select_reduce_fusion.1
  22.5 0.0 copy-done.6
  22.5 0.1 fusion.7
  22.6 32.8 %collective-permute-done.other = bf16[384,1024]{1,0:T(8,128)(2,1)} collective-permute-done((bf16[384,1024]{1,0:T(8,128)(2,1)S(1)}, bf16[384,1024]{1,0:T(8,128)(2,1)}, u32[]{:S(2)}, u32[]{:S(2)}) %collective-permute-start) | collective-permute-done | bytes 786464 | tf_op jit(solution)/shard_map/ppermute | solution.py:14
  55.4 9.2 %collective-permute-start.1 = (bf16[192,1024]{1,0:T(8,128)(2,1)S(1)}, bf16[192,1024]{1,0:T(8,128)(2,1)S(1)}, u32[]{:S(2)}, u32[]{:S(2)}) collective-permute-start(bf16[192,1024]{1,0:T(8,128)(2,1)S(1)} %get-tuple-element.43), channel_id=1, source_target_pairs={{0,8},{1,9},{2,10},{3,11},{4,12},{5,13},{6,14},{7,15},{8,0},{9,1},... | collective-permute-start | bytes 1179656 | tf_op jit(solution)/shard_map/ppermute | solution.py:14
  64.6 1.9 %collective-permute-start.2 = (bf16[384,1024]{1,0:T(8,128)(2,1)}, bf16[384,1024]{1,0:T(8,128)(2,1)S(1)}, u32[]{:S(2)}, u32[]{:S(2)}) collective-permute-start(bf16[384,1024]{1,0:T(8,128)(2,1)} %get-tuple-element.46.own), channel_id=1, source_target_pairs={{0,1},{1,0},{2,3},{3,2},{4,5},{5,4},{6,7},{7,6},{8,9},{9,8},{10,11... | collective-permute-start | bytes 2359304 | tf_op jit(solution)/shard_map/ppermute | solution.py:14
  66.6 2.4 %collective-permute-start.3 = (bf16[384,1024]{1,0:T(8,128)(2,1)}, bf16[384,1024]{1,0:T(8,128)(2,1)S(1)}, u32[]{:S(2)}, u32[]{:S(2)}) collective-permute-start(bf16[384,1024]{1,0:T(8,128)(2,1)} %collective-permute-done.other), channel_id=1, source_target_pairs={{0,1},{1,0},{2,3},{3,2},{4,5},{5,4},{6,7},{7,6},{8,9},{9,8},{10,11... | collective-permute-start | bytes 2359304 | tf_op jit(solution)/shard_map/ppermute | solution.py:14
  69.0 1.9 %collective-permute-start.4 = (bf16[192,1024]{1,0:T(8,128)(2,1)S(1)}, bf16[192,1024]{1,0:T(8,128)(2,1)S(1)}, u32[]{:S(2)}, u32[]{:S(2)}) collective-permute-start(bf16[192,1024]{1,0:T(8,128)(2,1)S(1)} %get-tuple-element.47.own_down), channel_id=1, source_target_pairs={{0,1},{1,0},{2,3},{3,2},{4,5},{5,4},{6,7},{7,6},{8,9},{9,8},{10,11... | collective-permute-start | bytes 1179656 | tf_op jit(solution)/shard_map/ppermute | solution.py:14
  70.9 16.2 %all-gather.3.cloned.1.call-done = bf16[1,2048,1024]{2,1,0:T(8,128)(2,1)} async-done(((bf16[1,128,1024]{2,1,0:T(8,128)(2,1)}), bf16[1,2048,1024]{2,1,0:T(8,128)(2,1)}) %all-gather.3.cloned.1.call-update) | async-done | bytes 4194320 | tf_op jit(solution)/shard_map/all_gather | solution.py:178
  87.1 0.0 copy-start
  87.1 2.2 %copy-done = bf16[1,2048,1024]{2,1,0:T(8,128)(2,1)S(1)} copy-done((bf16[1,2048,1024]{2,1,0:T(8,128)(2,1)S(1)}, bf16[1,2048,1024]{2,1,0:T(8,128)(2,1)}, u32[]{:S(2)}) %copy-start) | copy-done | bytes 4194328
  89.3 0.0 copy-start.1
  89.3 6.9 %blend.1 = (bf16[384,1024]{1,0:T(8,128)(2,1)S(1)}, f32[192,128]{1,0:T(8,128)S(1)}) custom-call(s32[1]{0:T(128)} %bitcast.3.upper, f32[4,1,512]{2,1,0:T(1,128)S(1)} %bitcast.29, bf16[2048,1024]{1,0:T(8,128)(2,1)S(1)} %bitcast.21, bf16[384,1024]{1,0:T(8,128)(2,1)} %get-tuple-element.46.own, bf16[384,1024]{1,0:T(8,128)(2,1)} %collective-permute-done.other), custom_call_target="tpu_custom_call" | custom-call | flops 3221225472 | bytes 4194304 | tf_op jit(solution)/shard_map/blend/pallas_call | solution.py:218
  96.2 0.0 collective-permute-done.1.other_down
  96.2 2.1 %collective-permute-start.5 = (bf16[192,1024]{1,0:T(8,128)(2,1)S(1)}, bf16[192,1024]{1,0:T(8,128)(2,1)S(1)}, u32[]{:S(2)}, u32[]{:S(2)}) collective-permute-start(bf16[192,1024]{1,0:T(8,128)(2,1)S(1)} %collective-permute-done.1.other_down), channel_id=1, source_target_pairs={{0,1},{1,0},{2,3},{3,2},{4,5},{5,4},{6,7},{7,6},{8,9},{9,8},{10,11... | collective-permute-start | bytes 1179656 | tf_op jit(solution)/shard_map/ppermute | solution.py:14
  98.3 2.2 %collective-permute-start.6 = (f32[192,128]{1,0:T(8,128)S(1)}, f32[192,128]{1,0:T(8,128)S(1)}, u32[]{:S(2)}, u32[]{:S(2)}) collective-permute-start(f32[192,128]{1,0:T(8,128)S(1)} %get-tuple-element.48.blend), channel_id=1, source_target_pairs={{0,1},{1,0},{2,3},{3,2},{4,5},{5,4},{6,7},{7,6},{8,9},{9,8},{10,11... | collective-permute-start | bytes 294920 | tf_op jit(solution)/shard_map/ppermute | solution.py:14
  100.5 0.0 collective-permute-done.4.next_own_down
  100.5 0.0 collective-permute-done.2.next_own
  100.6 0.0 collective-permute-done.3.next_other
  100.6 1.0 collective-permute-done.6.next_blend
  101.5 0.0 collective-permute-done.5.next_down
  101.5 0.0 copy-done.1
  101.5 2.7 %first.1 = (bf16[64,1024]{1,0:T(8,128)(2,1)S(1)}, bf16[64,1024]{1,0:T(8,128)(2,1)S(1)}, bf16[128,1024]{1,0:T(8,128)(2,1)S(1)}, bf16[128,1024]{1,0:T(8,128)(2,1)S...) custom-call(s32[4]{0:T(128)S(1)} %get-tuple-element.36.places, ...), custom_call_target="tpu_custom_call" | custom-call | flops 603979776 | bytes 3932160 | tf_op jit(solution)/shard_map/first/pallas_call | solution.py:250
  104.2 3.7 %collective-permute-start.7 = (bf16[64,1024]{1,0:T(8,128)(2,1)S(1)}, bf16[64,1024]{1,0:T(8,128)(2,1)S(1)}, u32[]{:S(2)}, u32[]{:S(2)}) collective-permute-start(bf16[64,1024]{1,0:T(8,128)(2,1)S(1)} %get-tuple-element.52), channel_id=1, source_target_pairs={{0,2},{1,3},{2,4},{3,5},{4,6},{5,7},{6,8},{7,9},{8,10},{9,11},{10,... | collective-permute-start | bytes 393224 | tf_op jit(solution)/shard_map/ppermute | solution.py:14
  108.0 3.3 %collective-permute-start.8 = (bf16[64,1024]{1,0:T(8,128)(2,1)S(1)}, bf16[64,1024]{1,0:T(8,128)(2,1)S(1)}, u32[]{:S(2)}, u32[]{:S(2)}) collective-permute-start(bf16[64,1024]{1,0:T(8,128)(2,1)S(1)} %get-tuple-element.55), channel_id=1, source_target_pairs={{0,14},{1,15},{2,0},{3,1},{4,2},{5,3},{6,4},{7,5},{8,6},{9,7},{10,... | collective-permute-start | bytes 393224 | tf_op jit(solution)/shard_map/ppermute | solution.py:14
  111.3 2.7 %terms.1 = (bf16[128,1024]{1,0:T(8,128)(2,1)S(1)}, bf16[128,1024]{1,0:T(8,128)(2,1)S(1)}, bf16[128,1024]{1,0:T(8,128)(2,1)S(1)}, bf16[128,1024]{1,0:T(8,128)(2,1)S(1)}) custom-call(s32[4]{0:T(128)S(1)} %get-tuple-element.56.places, f32[16,2,128]{2,1,0:T(2,128)S(1)} %pad_maximum_fusion.2.weight_a.weight_b.weight_c.weight_d, ...), custom_call_target="tpu_custom_call" | custom-call | flops 603979776 | bytes 4194304 | tf_op jit(solution)/shard_map/terms/pallas_call | solution.py:267
  114.0 0.0 collective-permute-done.7
  114.1 6.8 %collective-permute-done.8 = bf16[64,1024]{1,0:T(8,128)(2,1)S(1)} collective-permute-done((bf16[64,1024]{1,0:T(8,128)(2,1)S(1)}, bf16[64,1024]{1,0:T(8,128)(2,1)S(1)}, u32[]{:S(2)}, u32[]{:S(2)}) %collective-permute-start.8) | collective-permute-done | bytes 131104 | tf_op jit(solution)/shard_map/ppermute | solution.py:14
  120.9 5.6 %collective-permute-start.9 = (bf16[128,1024]{1,0:T(8,128)(2,1)S(1)}, bf16[128,1024]{1,0:T(8,128)(2,1)S(1)}, u32[]{:S(2)}, u32[]{:S(2)}) collective-permute-start(bf16[128,1024]{1,0:T(8,128)(2,1)S(1)} %pad_maximum_fusion), channel_id=1, source_target_pairs={{0,2},{1,3},{2,4},{3,5},{4,6},{5,7},{6,8},{7,9},{8,10},{9,11},{10,... | collective-permute-start | bytes 786440 | tf_op jit(solution)/shard_map/ppermute | solution.py:14
  126.5 1.9 %collective-permute-start.11 = (bf16[128,1024]{1,0:T(8,128)(2,1)S(1)}, bf16[128,1024]{1,0:T(8,128)(2,1)S(1)}, u32[]{:S(2)}, u32[]{:S(2)}) collective-permute-start(bf16[128,1024]{1,0:T(8,128)(2,1)S(1)} %pad_maximum_fusion.1), channel_id=1, source_target_pairs={{0,14},{1,15},{2,0},{3,1},{4,2},{5,3},{6,4},{7,5},{8,6},{9,7},{10,... | collective-permute-start | bytes 786440 | tf_op jit(solution)/shard_map/ppermute | solution.py:14
  128.4 0.1 slice_bitcast_fusion
  128.5 0.0 copy-start.3
  128.5 4.1 %collective-permute-start.13 = (bf16[128,1024]{1,0:T(8,128)(2,1)S(1)}, bf16[128,1024]{1,0:T(8,128)(2,1)S(1)}, u32[]{:S(2)}, u32[]{:S(2)}) collective-permute-start(bf16[128,1024]{1,0:T(8,128)(2,1)S(1)} %get-tuple-element.64), channel_id=1, source_target_pairs={{0,2},{1,3},{2,4},{3,5},{4,6},{5,7},{6,8},{7,9},{8,10},{9,11},{10,... | collective-permute-start | bytes 786440 | tf_op jit(solution)/shard_map/ppermute | solution.py:14
  132.6 3.1 %collective-permute-start.14 = (bf16[128,1024]{1,0:T(8,128)(2,1)S(1)}, bf16[128,1024]{1,0:T(8,128)(2,1)S(1)}, u32[]{:S(2)}, u32[]{:S(2)}) collective-permute-start(bf16[128,1024]{1,0:T(8,128)(2,1)S(1)} %get-tuple-element.65), channel_id=1, source_target_pairs={{0,14},{1,15},{2,0},{3,1},{4,2},{5,3},{6,4},{7,5},{8,6},{9,7},{10,... | collective-permute-start | bytes 786440 | tf_op jit(solution)/shard_map/ppermute | solution.py:14
  135.7 0.0 collective-permute-done.9
  135.7 0.1 add_convert_fusion.2
  135.8 4.8 %collective-permute-start.10 = (bf16[128,1024]{1,0:T(8,128)(2,1)S(1)}, bf16[128,1024]{1,0:T(8,128)(2,1)S(1)}, u32[]{:S(2)}, u32[]{:S(2)}) collective-permute-start(bf16[128,1024]{1,0:T(8,128)(2,1)S(1)} %add_convert_fusion.2), channel_id=1, source_target_pairs={{0,20},{1,21},{2,22},{3,23},{4,24},{5,25},{6,26},{7,27},{8,28},{9,... | collective-permute-start | bytes 786440 | tf_op jit(solution)/shard_map/ppermute | solution.py:28
  140.6 0.0 collective-permute-done.11
  140.6 0.1 add_convert_fusion.1
  140.7 5.3 %collective-permute-start.12 = (bf16[128,1024]{1,0:T(8,128)(2,1)S(1)}, bf16[128,1024]{1,0:T(8,128)(2,1)S(1)}, u32[]{:S(2)}, u32[]{:S(2)}) collective-permute-start(bf16[128,1024]{1,0:T(8,128)(2,1)S(1)} %add_convert_fusion.1), channel_id=1, source_target_pairs={{0,28},{1,29},{2,30},{3,31},{4,16},{5,17},{6,18},{7,19},{8,20},{9,... | collective-permute-start | bytes 786440 | tf_op jit(solution)/shard_map/ppermute | solution.py:28
  145.9 0.0 collective-permute-done.13
  146.0 0.0 collective-permute-done.14
  146.0 0.0 copy-done.3
  146.0 0.2 fusion.2
  146.2 3.5 %collective-permute-start.15 = (bf16[128,1024]{1,0:T(8,128)(2,1)S(1)}, bf16[128,1024]{1,0:T(8,128)(2,1)S(1)}, u32[]{:S(2)}, u32[]{:S(2)}) collective-permute-start(bf16[128,1024]{1,0:T(8,128)(2,1)S(1)} %fusion.2), channel_id=1, source_target_pairs={{0,16},{1,17},{2,18},{3,19},{4,20},{5,21},{6,22},{7,23},{8,24},{9,... | collective-permute-start | bytes 786440 | tf_op jit(solution)/shard_map/ppermute | solution.py:28
  149.7 1.1 maximum_bitcast_fusion
  150.9 4.0 %collective-permute-done.10 = bf16[128,1024]{1,0:T(8,128)(2,1)S(1)} collective-permute-done((bf16[128,1024]{1,0:T(8,128)(2,1)S(1)}, bf16[128,1024]{1,0:T(8,128)(2,1)S(1)}, u32[]{:S(2)}, u32[]{:S(2)}) %collective-permute-start.10) | collective-permute-done | bytes 262176 | tf_op jit(solution)/shard_map/ppermute | solution.py:28
  154.8 7.8 %collective-permute-done.12 = bf16[128,1024]{1,0:T(8,128)(2,1)S(1)} collective-permute-done((bf16[128,1024]{1,0:T(8,128)(2,1)S(1)}, bf16[128,1024]{1,0:T(8,128)(2,1)S(1)}, u32[]{:S(2)}, u32[]{:S(2)}) %collective-permute-start.12) | collective-permute-done | bytes 262176 | tf_op jit(solution)/shard_map/ppermute | solution.py:28
  162.6 1.6 collective-permute-done.15
  164.2 0.8 fusion.3
  (9 shorter events, 0.2 us)
Async XLA Ops:
  7.2 79.9 %all-gather.3.cloned.1.call-start = ((), (), s32[]{:S(2)}) async-start(), calls=%async_computation | async-start | bytes 4456448 | tf_op jit(solution)/shard_map/all_gather | solution.py:178
  7.9 1.7 copy-start.2
  9.6 12.8 %copy-start.4 = (f32[1,2048,8]{1,2,0:T(8,128)S(1)}, f32[1,2048,8]{1,2,0:T(8,128)}, u32[]{:S(2)}) copy-start(f32[1,2048,8]{1,2,0:T(8,128)} %param.7) | copy-start | bytes 196612
  9.6 12.8 %copy-start.5 = (s32[1,2048,8]{1,2,0:T(8,128)S(1)}, s32[1,2048,8]{1,2,0:T(8,128)}, u32[]{:S(2)}) copy-start(s32[1,2048,8]{1,2,0:T(8,128)} %param.6) | copy-start | bytes 196612
  9.6 12.9 %copy-start.6 = (s32[8]{0:T(128)S(1)}, s32[8]{0:T(128)}, u32[]{:S(2)}) copy-start(s32[8]{0:T(128)} %constant.54.clone) | copy-start | bytes 100
  11.4 44.0 %collective-permute-start = (bf16[384,1024]{1,0:T(8,128)(2,1)S(1)}, bf16[384,1024]{1,0:T(8,128)(2,1)}, u32[]{:S(2)}, u32[]{:S(2)}) collective-permute-start(bf16[384,1024]{1,0:T(8,128)(2,1)S(1)} %get-tuple-element.40), channel_id=1, source_target_pairs={{0,8},{1,9},{2,10},{3,11},{4,12},{5,13},{6,14},{7,15},{8,0},{9,1},... | collective-permute-start | bytes 2359304 | tf_op jit(solution)/shard_map/ppermute | solution.py:14
  55.4 40.8 %collective-permute-start.1 = (bf16[192,1024]{1,0:T(8,128)(2,1)S(1)}, bf16[192,1024]{1,0:T(8,128)(2,1)S(1)}, u32[]{:S(2)}, u32[]{:S(2)}) collective-permute-start(bf16[192,1024]{1,0:T(8,128)(2,1)S(1)} %get-tuple-element.43), channel_id=1, source_target_pairs={{0,8},{1,9},{2,10},{3,11},{4,12},{5,13},{6,14},{7,15},{8,0},{9,1},... | collective-permute-start | bytes 1179656 | tf_op jit(solution)/shard_map/ppermute | solution.py:14
  64.6 35.9 %collective-permute-start.2 = (bf16[384,1024]{1,0:T(8,128)(2,1)}, bf16[384,1024]{1,0:T(8,128)(2,1)S(1)}, u32[]{:S(2)}, u32[]{:S(2)}) collective-permute-start(bf16[384,1024]{1,0:T(8,128)(2,1)} %get-tuple-element.46.own), channel_id=1, source_target_pairs={{0,1},{1,0},{2,3},{3,2},{4,5},{5,4},{6,7},{7,6},{8,9},{9,8},{10,11... | collective-permute-start | bytes 2359304 | tf_op jit(solution)/shard_map/ppermute | solution.py:14
  66.6 34.0 %collective-permute-start.3 = (bf16[384,1024]{1,0:T(8,128)(2,1)}, bf16[384,1024]{1,0:T(8,128)(2,1)S(1)}, u32[]{:S(2)}, u32[]{:S(2)}) collective-permute-start(bf16[384,1024]{1,0:T(8,128)(2,1)} %collective-permute-done.other), channel_id=1, source_target_pairs={{0,1},{1,0},{2,3},{3,2},{4,5},{5,4},{6,7},{7,6},{8,9},{9,8},{10,11... | collective-permute-start | bytes 2359304 | tf_op jit(solution)/shard_map/ppermute | solution.py:14
  69.0 31.6 %collective-permute-start.4 = (bf16[192,1024]{1,0:T(8,128)(2,1)S(1)}, bf16[192,1024]{1,0:T(8,128)(2,1)S(1)}, u32[]{:S(2)}, u32[]{:S(2)}) collective-permute-start(bf16[192,1024]{1,0:T(8,128)(2,1)S(1)} %get-tuple-element.47.own_down), channel_id=1, source_target_pairs={{0,1},{1,0},{2,3},{3,2},{4,5},{5,4},{6,7},{7,6},{8,9},{9,8},{10,11... | collective-permute-start | bytes 1179656 | tf_op jit(solution)/shard_map/ppermute | solution.py:14
  87.1 2.2 %copy-start = (bf16[1,2048,1024]{2,1,0:T(8,128)(2,1)S(1)}, bf16[1,2048,1024]{2,1,0:T(8,128)(2,1)}, u32[]{:S(2)}) copy-start(bf16[1,2048,1024]{2,1,0:T(8,128)(2,1)} %all-gather.3.cloned.1.call-done) | copy-start | bytes 12582916
  89.3 12.3 %copy-start.1 = (bf16[1,2048,1024]{2,1,0:T(8,128)(2,1)S(1)}, bf16[1,2048,1024]{2,1,0:T(8,128)(2,1)}, u32[]{:S(2)}) copy-start(bf16[1,2048,1024]{2,1,0:T(8,128)(2,1)} %all-gather.3.cloned.1.call-done) | copy-start | bytes 12582916
  96.2 5.3 %collective-permute-start.5 = (bf16[192,1024]{1,0:T(8,128)(2,1)S(1)}, bf16[192,1024]{1,0:T(8,128)(2,1)S(1)}, u32[]{:S(2)}, u32[]{:S(2)}) collective-permute-start(bf16[192,1024]{1,0:T(8,128)(2,1)S(1)} %collective-permute-done.1.other_down), channel_id=1, source_target_pairs={{0,1},{1,0},{2,3},{3,2},{4,5},{5,4},{6,7},{7,6},{8,9},{9,8},{10,11... | collective-permute-start | bytes 1179656 | tf_op jit(solution)/shard_map/ppermute | solution.py:14
  98.3 3.2 %collective-permute-start.6 = (f32[192,128]{1,0:T(8,128)S(1)}, f32[192,128]{1,0:T(8,128)S(1)}, u32[]{:S(2)}, u32[]{:S(2)}) collective-permute-start(f32[192,128]{1,0:T(8,128)S(1)} %get-tuple-element.48.blend), channel_id=1, source_target_pairs={{0,1},{1,0},{2,3},{3,2},{4,5},{5,4},{6,7},{7,6},{8,9},{9,8},{10,11... | collective-permute-start | bytes 294920 | tf_op jit(solution)/shard_map/ppermute | solution.py:14
  104.2 9.8 %collective-permute-start.7 = (bf16[64,1024]{1,0:T(8,128)(2,1)S(1)}, bf16[64,1024]{1,0:T(8,128)(2,1)S(1)}, u32[]{:S(2)}, u32[]{:S(2)}) collective-permute-start(bf16[64,1024]{1,0:T(8,128)(2,1)S(1)} %get-tuple-element.52), channel_id=1, source_target_pairs={{0,2},{1,3},{2,4},{3,5},{4,6},{5,7},{6,8},{7,9},{8,10},{9,11},{10,... | collective-permute-start | bytes 393224 | tf_op jit(solution)/shard_map/ppermute | solution.py:14
  108.0 12.9 %collective-permute-start.8 = (bf16[64,1024]{1,0:T(8,128)(2,1)S(1)}, bf16[64,1024]{1,0:T(8,128)(2,1)S(1)}, u32[]{:S(2)}, u32[]{:S(2)}) collective-permute-start(bf16[64,1024]{1,0:T(8,128)(2,1)S(1)} %get-tuple-element.55), channel_id=1, source_target_pairs={{0,14},{1,15},{2,0},{3,1},{4,2},{5,3},{6,4},{7,5},{8,6},{9,7},{10,... | collective-permute-start | bytes 393224 | tf_op jit(solution)/shard_map/ppermute | solution.py:14
  120.9 14.8 %collective-permute-start.9 = (bf16[128,1024]{1,0:T(8,128)(2,1)S(1)}, bf16[128,1024]{1,0:T(8,128)(2,1)S(1)}, u32[]{:S(2)}, u32[]{:S(2)}) collective-permute-start(bf16[128,1024]{1,0:T(8,128)(2,1)S(1)} %pad_maximum_fusion), channel_id=1, source_target_pairs={{0,2},{1,3},{2,4},{3,5},{4,6},{5,7},{6,8},{7,9},{8,10},{9,11},{10,... | collective-permute-start | bytes 786440 | tf_op jit(solution)/shard_map/ppermute | solution.py:14
  126.5 14.1 %collective-permute-start.11 = (bf16[128,1024]{1,0:T(8,128)(2,1)S(1)}, bf16[128,1024]{1,0:T(8,128)(2,1)S(1)}, u32[]{:S(2)}, u32[]{:S(2)}) collective-permute-start(bf16[128,1024]{1,0:T(8,128)(2,1)S(1)} %pad_maximum_fusion.1), channel_id=1, source_target_pairs={{0,14},{1,15},{2,0},{3,1},{4,2},{5,3},{6,4},{7,5},{8,6},{9,7},{10,... | collective-permute-start | bytes 786440 | tf_op jit(solution)/shard_map/ppermute | solution.py:14
  128.5 17.5 %copy-start.3 = (bf16[1,128,1024]{2,1,0:T(8,128)(2,1)S(1)}, bf16[1,128,1024]{2,1,0:T(8,128)(2,1)}, u32[]{:S(2)}) copy-start(bf16[1,128,1024]{2,1,0:T(8,128)(2,1)} %param.5) | copy-start | bytes 786436
  128.5 17.4 %collective-permute-start.13 = (bf16[128,1024]{1,0:T(8,128)(2,1)S(1)}, bf16[128,1024]{1,0:T(8,128)(2,1)S(1)}, u32[]{:S(2)}, u32[]{:S(2)}) collective-permute-start(bf16[128,1024]{1,0:T(8,128)(2,1)S(1)} %get-tuple-element.64), channel_id=1, source_target_pairs={{0,2},{1,3},{2,4},{3,5},{4,6},{5,7},{6,8},{7,9},{8,10},{9,11},{10,... | collective-permute-start | bytes 786440 | tf_op jit(solution)/shard_map/ppermute | solution.py:14
  132.6 13.4 %collective-permute-start.14 = (bf16[128,1024]{1,0:T(8,128)(2,1)S(1)}, bf16[128,1024]{1,0:T(8,128)(2,1)S(1)}, u32[]{:S(2)}, u32[]{:S(2)}) collective-permute-start(bf16[128,1024]{1,0:T(8,128)(2,1)S(1)} %get-tuple-element.65), channel_id=1, source_target_pairs={{0,14},{1,15},{2,0},{3,1},{4,2},{5,3},{6,4},{7,5},{8,6},{9,7},{10,... | collective-permute-start | bytes 786440 | tf_op jit(solution)/shard_map/ppermute | solution.py:14
  135.8 19.0 %collective-permute-start.10 = (bf16[128,1024]{1,0:T(8,128)(2,1)S(1)}, bf16[128,1024]{1,0:T(8,128)(2,1)S(1)}, u32[]{:S(2)}, u32[]{:S(2)}) collective-permute-start(bf16[128,1024]{1,0:T(8,128)(2,1)S(1)} %add_convert_fusion.2), channel_id=1, source_target_pairs={{0,20},{1,21},{2,22},{3,23},{4,24},{5,25},{6,26},{7,27},{8,28},{9,... | collective-permute-start | bytes 786440 | tf_op jit(solution)/shard_map/ppermute | solution.py:28
  140.7 21.9 %collective-permute-start.12 = (bf16[128,1024]{1,0:T(8,128)(2,1)S(1)}, bf16[128,1024]{1,0:T(8,128)(2,1)S(1)}, u32[]{:S(2)}, u32[]{:S(2)}) collective-permute-start(bf16[128,1024]{1,0:T(8,128)(2,1)S(1)} %add_convert_fusion.1), channel_id=1, source_target_pairs={{0,28},{1,29},{2,30},{3,31},{4,16},{5,17},{6,18},{7,19},{8,20},{9,... | collective-permute-start | bytes 786440 | tf_op jit(solution)/shard_map/ppermute | solution.py:28
  146.2 18.0 %collective-permute-start.15 = (bf16[128,1024]{1,0:T(8,128)(2,1)S(1)}, bf16[128,1024]{1,0:T(8,128)(2,1)S(1)}, u32[]{:S(2)}, u32[]{:S(2)}) collective-permute-start(bf16[128,1024]{1,0:T(8,128)(2,1)S(1)} %fusion.2), channel_id=1, source_target_pairs={{0,16},{1,17},{2,18},{3,19},{4,20},{5,21},{6,22},{7,23},{8,24},{9,... | collective-permute-start | bytes 786440 | tf_op jit(solution)/shard_map/ppermute | solution.py:28
Sparse Core Ops, SparseCore 0:
  10.1 76.9 all-gather.2

commit v3 on v2

--- a/solution.py
+++ b/solution.py
@@ -194,8 +194,6 @@
     partner_in = along(send_in, count, across)
     send_down, partner_in = lax.optimization_barrier((send_down, partner_in))
     partner_down = along(send_down, count, across)
-    next_other = along(partner_in, count, sibling)
-
     members, row_weight = [], []
     for pair in (me % pair_count, (me % pair_count) ^ 1):
         named = (layer_routes == pair) | (layer_routes == pair + pair_count)
@@ -210,6 +208,8 @@
     )
     next_own = along(kept_in, count, sibling)
     next_own_down = along(kept_down, count, sibling)
+    next_own, next_own_down, swapped = lax.optimization_barrier((next_own, next_own_down, partner_in))
+    next_other = along(swapped, count, sibling)
 
     whole = lambda shape: pl.BlockSpec(shape, lambda i, *_: (0,) * len(shape))
     held = pl.BlockSpec(memory_space=pltpu.VMEM)
@@ -223,8 +223,8 @@
             in_specs=[
                 pl.BlockSpec((1, 1, group), lambda i, *_: (i, 0, 0)),
                 pl.BlockSpec((group, features), lambda i, *_: (i, 0)),
-                held,
-                held,
+                whole((2 * units, features)),
+                whole((2 * units, features)),
             ],
             out_specs=[whole((2 * units, features)), whole((units, 128))],
             scratch_shapes=[pltpu.VMEM((3, units, 128), jnp.float32), pltpu.VMEM((1, 128), jnp.float32)],
@@ -287,7 +287,8 @@
     three, minus_three = terms[far - 1], terms[chips - far + 1]
     grown = jnp.concatenate([add(behind, three[:half]), three[half:]], axis=0)
     minus_grown = jnp.concatenate([minus_three[:half], add(ahead, minus_three[half:])], axis=0)
-    grown, minus_grown, one, minus_one = lax.optimization_barrier((grown, minus_grown, terms[1], terms[chips - 1]))
+    one = terms[1]
+    grown, minus_grown, minus_one = lax.optimization_barrier((grown, minus_grown, terms[chips - 1]))
     grown = add(along(grown, count, ring(count, 1)), terms[far - 2])
     minus_grown = add(along(minus_grown, count, ring(count, -1)), terms[chips - far + 2])
     here = add(x_local, terms[0], along(one, count, ring(count, 1)), along(minus_one, count, ring(count, -1)))

time: 172 us -> 171 us (level); the launches traced: 172 us -> 169 us
  waiting for transfers between devices: 70.7 us -> 64 us
  local copies, waits for them, and re-layouts: 4.04 us -> 8.83 us
    ppermute x13, waiting for transfers between devices: 40.6 us -> 34.9 us  [along(): return lax.ppermute(array, 'expert', [(i, target(i)) for i in range(count)])]
    unnamed x14 -> x24, local copies, waits for them, and re-layouts: 3.87 us -> 8.65 us
  transfers between devices with their start and end apart: 17 -> 17, of which waited for: 7 -> 7; matrix products, arithmetic and copies ran while one was open for 1% -> 1% of each run, Pallas kernels for 7% -> 6%
where the time goes in v3:
time: 171 us; the launch traced here: 169 us
  starting transfers between devices  66.2 us (39%)
  waiting for transfers between devices  64 us (37%)
  between operations  14.5 us (8%)
  Pallas kernels  12.6 us (7%)
  local copies, waits for them, and re-layouts  8.83 us (5%)
  other arithmetic  2.48 us (1%)
    ppermute x13, starting transfers between devices, along(): return lax.ppermute(array, 'expert', [(i, target(i)) for i in range(count)])  52.4 us
    ppermute x13, waiting for transfers between devices, along(): return lax.ppermute(array, 'expert', [(i, target(i)) for i in range(count)])  34.9 us
    all_gather x1, waiting for transfers between devices, local(): x_all = lax.all_gather(x_local, 'expert', axis=0, tiled=True)  15.5 us
    ppermute x3, starting transfers between devices, next_layer(): return lax.ppermute(array, ('section', 'expert'), route)  13.8 us
    ppermute x3, waiting for transfers between devices, next_layer(): return lax.ppermute(array, ('section', 'expert'), route)  12.9 us
    unnamed x24, local copies, waits for them, and re-layouts  8.65 us
    pallas_call x1, Pallas kernels, local(): pl.pallas_call(blend_kernel, grid_spec=pltpu.PrefetchScalarGridSpec(num_s...  5.39 us
  transfers between devices with their start and end apart: 17, of which 7 were waited for; matrix products, arithmetic and copies ran while one was open for 1% of the time, Pallas kernels for 6%

profile of v3, /device:TPU:6, one launch (start us, length us, event | category | flops | bytes accessed | tf_op | source)
XLA Modules:
  0.0 168.6 jit_solution(7065697943772464116)
XLA Ops:
  7.2 0.0 all-gather.3.cloned.1.call-start
  7.2 0.7 all-gather.3.cloned.1.call-update
  7.9 0.0 copy-start.2
  7.9 1.7 copy-done.2
  9.6 0.0 copy-start.9
  9.6 0.0 copy-start.10
  9.6 1.9 %split.1 = (bf16[384,1024]{1,0:T(8,128)(2,1)S(1)}, bf16[192,1024]{1,0:T(8,128)(2,1)S(1)}, bf16[384,1024]{1,0:T(8,128)(2,1)}, bf16[192,1024]{1,0:T(8,128)(2,1)S(1)}) custom-call(s32[1]{0:T(128)} %bitcast.3.upper, bf16[3,1024,384]{2,1,0:T(8,128)(2,1)S(1)} %bitcast.28), custom_call_target="tpu_custom_call" | custom-call | bytes 4718592 | tf_op jit(solution)/shard_map/split/pallas_call | solution.py:181
  11.4 0.8 copy-done.7
  12.2 10.9 %collective-permute-start = (bf16[384,1024]{1,0:T(8,128)(2,1)}, bf16[384,1024]{1,0:T(8,128)(2,1)S(1)}, u32[]{:S(2)}, u32[]{:S(2)}) collective-permute-start(bf16[384,1024]{1,0:T(8,128)(2,1)} %get-tuple-element.42), channel_id=1, source_target_pairs={{0,8},{1,9},{2,10},{3,11},{4,12},{5,13},{6,14},{7,15},{8,0},{9,1},... | collective-permute-start | bytes 2359304 | tf_op jit(solution)/shard_map/ppermute | solution.py:14
  23.1 0.0 copy-done.9
  23.2 0.0 copy-done.10
  23.2 0.1 select_reduce_fusion.1
  23.3 0.0 copy-done.11
  23.3 0.1 fusion.7
  23.4 1.9 %collective-permute-start.2 = (bf16[384,1024]{1,0:T(8,128)(2,1)S(1)}, bf16[384,1024]{1,0:T(8,128)(2,1)S(1)}, u32[]{:S(2)}, u32[]{:S(2)}) collective-permute-start(bf16[384,1024]{1,0:T(8,128)(2,1)S(1)} %get-tuple-element.48.own), channel_id=1, source_target_pairs={{0,1},{1,0},{2,3},{3,2},{4,5},{5,4},{6,7},{7,6},{8,9},{9,8},{10,11... | collective-permute-start | bytes 2359304 | tf_op jit(solution)/shard_map/ppermute | solution.py:14
  25.3 0.0 copy-start.5
  25.3 0.9 copy-done.5
  26.2 2.4 %collective-permute-start.3 = (bf16[192,1024]{1,0:T(8,128)(2,1)S(1)}, bf16[192,1024]{1,0:T(8,128)(2,1)S(1)}, u32[]{:S(2)}, u32[]{:S(2)}) collective-permute-start(bf16[192,1024]{1,0:T(8,128)(2,1)S(1)} %get-tuple-element.49.own_down), channel_id=1, source_target_pairs={{0,1},{1,0},{2,3},{3,2},{4,5},{5,4},{6,7},{7,6},{8,9},{9,8},{10,11... | collective-permute-start | bytes 1179656 | tf_op jit(solution)/shard_map/ppermute | solution.py:14
  28.6 29.8 %collective-permute-done.other = bf16[384,1024]{1,0:T(8,128)(2,1)S(1)} collective-permute-done((bf16[384,1024]{1,0:T(8,128)(2,1)}, bf16[384,1024]{1,0:T(8,128)(2,1)S(1)}, u32[]{:S(2)}, u32[]{:S(2)}) %collective-permute-start) | collective-permute-done | bytes 786464 | tf_op jit(solution)/shard_map/ppermute | solution.py:14
  58.4 0.9 copy-done.3
  59.3 9.0 %collective-permute-start.1 = (bf16[192,1024]{1,0:T(8,128)(2,1)}, bf16[192,1024]{1,0:T(8,128)(2,1)S(1)}, u32[]{:S(2)}, u32[]{:S(2)}) collective-permute-start(bf16[192,1024]{1,0:T(8,128)(2,1)} %copy-done.7), channel_id=1, source_target_pairs={{0,8},{1,9},{2,10},{3,11},{4,12},{5,13},{6,14},{7,15},{8,0},{9,1},... | collective-permute-start | bytes 1179656 | tf_op jit(solution)/shard_map/ppermute | solution.py:14
  68.3 0.0 collective-permute-done.3.next_own_down
  68.3 0.0 collective-permute-done.2.next_own
  68.3 1.9 %collective-permute-start.4 = (bf16[384,1024]{1,0:T(8,128)(2,1)}, bf16[384,1024]{1,0:T(8,128)(2,1)S(1)}, u32[]{:S(2)}, u32[]{:S(2)}) collective-permute-start(bf16[384,1024]{1,0:T(8,128)(2,1)} %copy-done.3), channel_id=1, source_target_pairs={{0,1},{1,0},{2,3},{3,2},{4,5},{5,4},{6,7},{7,6},{8,9},{9,8},{10,11... | collective-permute-start | bytes 2359304 | tf_op jit(solution)/shard_map/ppermute | solution.py:14
  70.3 15.5 %all-gather.3.cloned.1.call-done = bf16[1,2048,1024]{2,1,0:T(8,128)(2,1)} async-done(((bf16[1,128,1024]{2,1,0:T(8,128)(2,1)}), bf16[1,2048,1024]{2,1,0:T(8,128)(2,1)}) %all-gather.3.cloned.1.call-update) | async-done | bytes 4194320 | tf_op jit(solution)/shard_map/all_gather | solution.py:178
  85.8 2.2 %copy-done = bf16[1,2048,1024]{2,1,0:T(8,128)(2,1)S(1)} copy-done((bf16[1,2048,1024]{2,1,0:T(8,128)(2,1)S(1)}, bf16[1,2048,1024]{2,1,0:T(8,128)(2,1)}, u32[]{:S(2)}) %copy-start) | copy-done | bytes 4194328
  88.0 1.1 copy-done.4
  89.1 1.1 copy-done.6
  90.3 5.4 %blend.1 = (bf16[384,1024]{1,0:T(8,128)(2,1)S(1)}, f32[192,128]{1,0:T(8,128)S(1)}) custom-call(s32[1]{0:T(128)} %bitcast.3.upper, f32[4,1,512]{2,1,0:T(1,128)S(1)} %bitcast.29, bf16[2048,1024]{1,0:T(8,128)(2,1)S(1)} %bitcast.21, bf16[384,1024]{1,0:T(8,128)(2,1)S(1)} %copy-done.6, bf16[384,1024]{1,0:T(8,128)(2,1)S(1)} %copy-done.4), custom_call_target="tpu_custom_call" | custom-call | flops 3221225472 | bytes 4194304 | tf_op jit(solution)/shard_map/blend/pallas_call | solution.py:218
  95.7 0.0 collective-permute-done.1.other_down
  95.7 2.1 %collective-permute-start.5 = (bf16[192,1024]{1,0:T(8,128)(2,1)S(1)}, bf16[192,1024]{1,0:T(8,128)(2,1)S(1)}, u32[]{:S(2)}, u32[]{:S(2)}) collective-permute-start(bf16[192,1024]{1,0:T(8,128)(2,1)S(1)} %collective-permute-done.1.other_down), channel_id=1, source_target_pairs={{0,1},{1,0},{2,3},{3,2},{4,5},{5,4},{6,7},{7,6},{8,9},{9,8},{10,11... | collective-permute-start | bytes 1179656 | tf_op jit(solution)/shard_map/ppermute | solution.py:14
  97.8 2.2 %collective-permute-start.6 = (f32[192,128]{1,0:T(8,128)S(1)}, f32[192,128]{1,0:T(8,128)S(1)}, u32[]{:S(2)}, u32[]{:S(2)}) collective-permute-start(f32[192,128]{1,0:T(8,128)S(1)} %get-tuple-element.53.blend), channel_id=1, source_target_pairs={{0,1},{1,0},{2,3},{3,2},{4,5},{5,4},{6,7},{7,6},{8,9},{9,8},{10,11... | collective-permute-start | bytes 294920 | tf_op jit(solution)/shard_map/ppermute | solution.py:14
  100.0 0.0 collective-permute-done.4.next_other
  100.0 1.0 collective-permute-done.6.next_blend
  101.0 0.0 collective-permute-done.5.next_down
  101.0 0.0 copy-done.1
  101.0 2.7 %first.1 = (bf16[64,1024]{1,0:T(8,128)(2,1)S(1)}, bf16[64,1024]{1,0:T(8,128)(2,1)S(1)}, bf16[128,1024]{1,0:T(8,128)(2,1)S(1)}, bf16[128,1024]{1,0:T(8,128)(2,1)S...) custom-call(s32[4]{0:T(128)S(1)} %get-tuple-element.38.places, ...), custom_call_target="tpu_custom_call" | custom-call | flops 603979776 | bytes 3932160 | tf_op jit(solution)/shard_map/first/pallas_call | solution.py:250
  103.7 4.9 %collective-permute-start.7 = (bf16[64,1024]{1,0:T(8,128)(2,1)S(1)}, bf16[64,1024]{1,0:T(8,128)(2,1)S(1)}, u32[]{:S(2)}, u32[]{:S(2)}) collective-permute-start(bf16[64,1024]{1,0:T(8,128)(2,1)S(1)} %get-tuple-element.57), channel_id=1, source_target_pairs={{0,2},{1,3},{2,4},{3,5},{4,6},{5,7},{6,8},{7,9},{8,10},{9,11},{10,... | collective-permute-start | bytes 393224 | tf_op jit(solution)/shard_map/ppermute | solution.py:14
  108.6 2.2 %collective-permute-start.8 = (bf16[64,1024]{1,0:T(8,128)(2,1)S(1)}, bf16[64,1024]{1,0:T(8,128)(2,1)S(1)}, u32[]{:S(2)}, u32[]{:S(2)}) collective-permute-start(bf16[64,1024]{1,0:T(8,128)(2,1)S(1)} %get-tuple-element.60), channel_id=1, source_target_pairs={{0,14},{1,15},{2,0},{3,1},{4,2},{5,3},{6,4},{7,5},{8,6},{9,7},{10,... | collective-permute-start | bytes 393224 | tf_op jit(solution)/shard_map/ppermute | solution.py:14
  110.8 2.7 %terms.1 = (bf16[128,1024]{1,0:T(8,128)(2,1)S(1)}, bf16[128,1024]{1,0:T(8,128)(2,1)S(1)}, bf16[128,1024]{1,0:T(8,128)(2,1)S(1)}, bf16[128,1024]{1,0:T(8,128)(2,1)S(1)}) custom-call(s32[4]{0:T(128)S(1)} %get-tuple-element.61.places, f32[16,2,128]{2,1,0:T(2,128)S(1)} %pad_maximum_fusion.2.weight_a.weight_b.weight_c.weight_d, ...), custom_call_target="tpu_custom_call" | custom-call | flops 603979776 | bytes 4194304 | tf_op jit(solution)/shard_map/terms/pallas_call | solution.py:267
  113.5 0.0 collective-permute-done.7
  113.6 4.0 %collective-permute-done.8 = bf16[64,1024]{1,0:T(8,128)(2,1)S(1)} collective-permute-done((bf16[64,1024]{1,0:T(8,128)(2,1)S(1)}, bf16[64,1024]{1,0:T(8,128)(2,1)S(1)}, u32[]{:S(2)}, u32[]{:S(2)}) %collective-permute-start.8) | collective-permute-done | bytes 131104 | tf_op jit(solution)/shard_map/ppermute | solution.py:14
  117.7 5.8 %collective-permute-start.9 = (bf16[128,1024]{1,0:T(8,128)(2,1)S(1)}, bf16[128,1024]{1,0:T(8,128)(2,1)S(1)}, u32[]{:S(2)}, u32[]{:S(2)}) collective-permute-start(bf16[128,1024]{1,0:T(8,128)(2,1)S(1)} %pad_maximum_fusion), channel_id=1, source_target_pairs={{0,2},{1,3},{2,4},{3,5},{4,6},{5,7},{6,8},{7,9},{8,10},{9,11},{10,... | collective-permute-start | bytes 786440 | tf_op jit(solution)/shard_map/ppermute | solution.py:14
  123.4 1.9 %collective-permute-start.11 = (bf16[128,1024]{1,0:T(8,128)(2,1)S(1)}, bf16[128,1024]{1,0:T(8,128)(2,1)S(1)}, u32[]{:S(2)}, u32[]{:S(2)}) collective-permute-start(bf16[128,1024]{1,0:T(8,128)(2,1)S(1)} %pad_maximum_fusion.1), channel_id=1, source_target_pairs={{0,14},{1,15},{2,0},{3,1},{4,2},{5,3},{6,4},{7,5},{8,6},{9,7},{10,... | collective-permute-start | bytes 786440 | tf_op jit(solution)/shard_map/ppermute | solution.py:14
  125.3 0.1 slice_bitcast_fusion
  125.4 0.0 copy-start.8
  125.4 4.1 %collective-permute-start.13 = (bf16[128,1024]{1,0:T(8,128)(2,1)S(1)}, bf16[128,1024]{1,0:T(8,128)(2,1)S(1)}, u32[]{:S(2)}, u32[]{:S(2)}) collective-permute-start(bf16[128,1024]{1,0:T(8,128)(2,1)S(1)} %get-tuple-element.68), channel_id=1, source_target_pairs={{0,2},{1,3},{2,4},{3,5},{4,6},{5,7},{6,8},{7,9},{8,10},{9,11},{10,... | collective-permute-start | bytes 786440 | tf_op jit(solution)/shard_map/ppermute | solution.py:14
  129.5 3.1 %collective-permute-start.14 = (bf16[128,1024]{1,0:T(8,128)(2,1)S(1)}, bf16[128,1024]{1,0:T(8,128)(2,1)S(1)}, u32[]{:S(2)}, u32[]{:S(2)}) collective-permute-start(bf16[128,1024]{1,0:T(8,128)(2,1)S(1)} %get-tuple-element.69), channel_id=1, source_target_pairs={{0,14},{1,15},{2,0},{3,1},{4,2},{5,3},{6,4},{7,5},{8,6},{9,7},{10,... | collective-permute-start | bytes 786440 | tf_op jit(solution)/shard_map/ppermute | solution.py:14
  132.6 0.0 collective-permute-done.9
  132.6 0.1 add_convert_fusion.2
  132.7 4.8 %collective-permute-start.10 = (bf16[128,1024]{1,0:T(8,128)(2,1)S(1)}, bf16[128,1024]{1,0:T(8,128)(2,1)S(1)}, u32[]{:S(2)}, u32[]{:S(2)}) collective-permute-start(bf16[128,1024]{1,0:T(8,128)(2,1)S(1)} %add_convert_fusion.2), channel_id=1, source_target_pairs={{0,20},{1,21},{2,22},{3,23},{4,24},{5,25},{6,26},{7,27},{8,28},{9,... | collective-permute-start | bytes 786440 | tf_op jit(solution)/shard_map/ppermute | solution.py:28
  137.5 0.0 collective-permute-done.11
  137.5 0.1 add_convert_fusion.1
  137.6 5.6 %collective-permute-start.12 = (bf16[128,1024]{1,0:T(8,128)(2,1)S(1)}, bf16[128,1024]{1,0:T(8,128)(2,1)S(1)}, u32[]{:S(2)}, u32[]{:S(2)}) collective-permute-start(bf16[128,1024]{1,0:T(8,128)(2,1)S(1)} %add_convert_fusion.1), channel_id=1, source_target_pairs={{0,28},{1,29},{2,30},{3,31},{4,16},{5,17},{6,18},{7,19},{8,20},{9,... | collective-permute-start | bytes 786440 | tf_op jit(solution)/shard_map/ppermute | solution.py:28
  143.2 0.0 collective-permute-done.13
  143.2 0.0 collective-permute-done.14
  143.2 0.0 copy-done.8
  143.2 0.2 fusion.2
  143.4 3.4 %collective-permute-start.15 = (bf16[128,1024]{1,0:T(8,128)(2,1)S(1)}, bf16[128,1024]{1,0:T(8,128)(2,1)S(1)}, u32[]{:S(2)}, u32[]{:S(2)}) collective-permute-start(bf16[128,1024]{1,0:T(8,128)(2,1)S(1)} %fusion.2), channel_id=1, source_target_pairs={{0,16},{1,17},{2,18},{3,19},{4,20},{5,21},{6,22},{7,23},{8,24},{9,... | collective-permute-start | bytes 786440 | tf_op jit(solution)/shard_map/ppermute | solution.py:28
  146.8 1.1 maximum_bitcast_fusion
  148.0 3.7 %collective-permute-done.10 = bf16[128,1024]{1,0:T(8,128)(2,1)S(1)} collective-permute-done((bf16[128,1024]{1,0:T(8,128)(2,1)S(1)}, bf16[128,1024]{1,0:T(8,128)(2,1)S(1)}, u32[]{:S(2)}, u32[]{:S(2)}) %collective-permute-start.10) | collective-permute-done | bytes 262176 | tf_op jit(solution)/shard_map/ppermute | solution.py:28
  151.7 7.5 %collective-permute-done.12 = bf16[128,1024]{1,0:T(8,128)(2,1)S(1)} collective-permute-done((bf16[128,1024]{1,0:T(8,128)(2,1)S(1)}, bf16[128,1024]{1,0:T(8,128)(2,1)S(1)}, u32[]{:S(2)}, u32[]{:S(2)}) %collective-permute-start.12) | collective-permute-done | bytes 262176 | tf_op jit(solution)/shard_map/ppermute | solution.py:28
  159.2 1.7 collective-permute-done.15
  160.9 0.8 fusion.3
  (16 shorter events, 0.2 us)
Async XLA Ops:
  7.2 78.6 %all-gather.3.cloned.1.call-start = ((), (), s32[]{:S(2)}) async-start(), calls=%async_computation | async-start | bytes 4456448 | tf_op jit(solution)/shard_map/all_gather | solution.py:178
  7.9 1.7 copy-start.2
  9.6 13.6 %copy-start.9 = (f32[1,2048,8]{1,2,0:T(8,128)S(1)}, f32[1,2048,8]{1,2,0:T(8,128)}, u32[]{:S(2)}) copy-start(f32[1,2048,8]{1,2,0:T(8,128)} %param.7) | copy-start | bytes 196612
  9.6 13.6 %copy-start.10 = (s32[1,2048,8]{1,2,0:T(8,128)S(1)}, s32[1,2048,8]{1,2,0:T(8,128)}, u32[]{:S(2)}) copy-start(s32[1,2048,8]{1,2,0:T(8,128)} %param.6) | copy-start | bytes 196612
  9.6 13.7 %copy-start.11 = (s32[8]{0:T(128)S(1)}, s32[8]{0:T(128)}, u32[]{:S(2)}) copy-start(s32[8]{0:T(128)} %constant.54.clone) | copy-start | bytes 100
  11.4 0.8 copy-start.7
  12.2 46.2 %collective-permute-start = (bf16[384,1024]{1,0:T(8,128)(2,1)}, bf16[384,1024]{1,0:T(8,128)(2,1)S(1)}, u32[]{:S(2)}, u32[]{:S(2)}) collective-permute-start(bf16[384,1024]{1,0:T(8,128)(2,1)} %get-tuple-element.42), channel_id=1, source_target_pairs={{0,8},{1,9},{2,10},{3,11},{4,12},{5,13},{6,14},{7,15},{8,0},{9,1},... | collective-permute-start | bytes 2359304 | tf_op jit(solution)/shard_map/ppermute | solution.py:14
  23.4 45.0 %collective-permute-start.2 = (bf16[384,1024]{1,0:T(8,128)(2,1)S(1)}, bf16[384,1024]{1,0:T(8,128)(2,1)S(1)}, u32[]{:S(2)}, u32[]{:S(2)}) collective-permute-start(bf16[384,1024]{1,0:T(8,128)(2,1)S(1)} %get-tuple-element.48.own), channel_id=1, source_target_pairs={{0,1},{1,0},{2,3},{3,2},{4,5},{5,4},{6,7},{7,6},{8,9},{9,8},{10,11... | collective-permute-start | bytes 2359304 | tf_op jit(solution)/shard_map/ppermute | solution.py:14
  25.3 0.9 copy-start.5
  26.2 42.1 %collective-permute-start.3 = (bf16[192,1024]{1,0:T(8,128)(2,1)S(1)}, bf16[192,1024]{1,0:T(8,128)(2,1)S(1)}, u32[]{:S(2)}, u32[]{:S(2)}) collective-permute-start(bf16[192,1024]{1,0:T(8,128)(2,1)S(1)} %get-tuple-element.49.own_down), channel_id=1, source_target_pairs={{0,1},{1,0},{2,3},{3,2},{4,5},{5,4},{6,7},{7,6},{8,9},{9,8},{10,11... | collective-permute-start | bytes 1179656 | tf_op jit(solution)/shard_map/ppermute | solution.py:14
  58.4 0.9 copy-start.3
  59.3 36.4 %collective-permute-start.1 = (bf16[192,1024]{1,0:T(8,128)(2,1)}, bf16[192,1024]{1,0:T(8,128)(2,1)S(1)}, u32[]{:S(2)}, u32[]{:S(2)}) collective-permute-start(bf16[192,1024]{1,0:T(8,128)(2,1)} %copy-done.7), channel_id=1, source_target_pairs={{0,8},{1,9},{2,10},{3,11},{4,12},{5,13},{6,14},{7,15},{8,0},{9,1},... | collective-permute-start | bytes 1179656 | tf_op jit(solution)/shard_map/ppermute | solution.py:14
  68.3 31.7 %collective-permute-start.4 = (bf16[384,1024]{1,0:T(8,128)(2,1)}, bf16[384,1024]{1,0:T(8,128)(2,1)S(1)}, u32[]{:S(2)}, u32[]{:S(2)}) collective-permute-start(bf16[384,1024]{1,0:T(8,128)(2,1)} %copy-done.3), channel_id=1, source_target_pairs={{0,1},{1,0},{2,3},{3,2},{4,5},{5,4},{6,7},{7,6},{8,9},{9,8},{10,11... | collective-permute-start | bytes 2359304 | tf_op jit(solution)/shard_map/ppermute | solution.py:14
  85.8 2.2 %copy-start = (bf16[1,2048,1024]{2,1,0:T(8,128)(2,1)S(1)}, bf16[1,2048,1024]{2,1,0:T(8,128)(2,1)}, u32[]{:S(2)}) copy-start(bf16[1,2048,1024]{2,1,0:T(8,128)(2,1)} %all-gather.3.cloned.1.call-done) | copy-start | bytes 12582916
  88.0 1.1 copy-start.4
  89.1 1.1 copy-start.6
  90.3 10.8 %copy-start.1 = (bf16[1,2048,1024]{2,1,0:T(8,128)(2,1)S(1)}, bf16[1,2048,1024]{2,1,0:T(8,128)(2,1)}, u32[]{:S(2)}) copy-start(bf16[1,2048,1024]{2,1,0:T(8,128)(2,1)} %all-gather.3.cloned.1.call-done) | copy-start | bytes 12582916
  95.7 5.3 %collective-permute-start.5 = (bf16[192,1024]{1,0:T(8,128)(2,1)S(1)}, bf16[192,1024]{1,0:T(8,128)(2,1)S(1)}, u32[]{:S(2)}, u32[]{:S(2)}) collective-permute-start(bf16[192,1024]{1,0:T(8,128)(2,1)S(1)} %collective-permute-done.1.other_down), channel_id=1, source_target_pairs={{0,1},{1,0},{2,3},{3,2},{4,5},{5,4},{6,7},{7,6},{8,9},{9,8},{10,11... | collective-permute-start | bytes 1179656 | tf_op jit(solution)/shard_map/ppermute | solution.py:14
  97.8 3.2 %collective-permute-start.6 = (f32[192,128]{1,0:T(8,128)S(1)}, f32[192,128]{1,0:T(8,128)S(1)}, u32[]{:S(2)}, u32[]{:S(2)}) collective-permute-start(f32[192,128]{1,0:T(8,128)S(1)} %get-tuple-element.53.blend), channel_id=1, source_target_pairs={{0,1},{1,0},{2,3},{3,2},{4,5},{5,4},{6,7},{7,6},{8,9},{9,8},{10,11... | collective-permute-start | bytes 294920 | tf_op jit(solution)/shard_map/ppermute | solution.py:14
  103.7 9.8 %collective-permute-start.7 = (bf16[64,1024]{1,0:T(8,128)(2,1)S(1)}, bf16[64,1024]{1,0:T(8,128)(2,1)S(1)}, u32[]{:S(2)}, u32[]{:S(2)}) collective-permute-start(bf16[64,1024]{1,0:T(8,128)(2,1)S(1)} %get-tuple-element.57), channel_id=1, source_target_pairs={{0,2},{1,3},{2,4},{3,5},{4,6},{5,7},{6,8},{7,9},{8,10},{9,11},{10,... | collective-permute-start | bytes 393224 | tf_op jit(solution)/shard_map/ppermute | solution.py:14
  108.6 9.0 %collective-permute-start.8 = (bf16[64,1024]{1,0:T(8,128)(2,1)S(1)}, bf16[64,1024]{1,0:T(8,128)(2,1)S(1)}, u32[]{:S(2)}, u32[]{:S(2)}) collective-permute-start(bf16[64,1024]{1,0:T(8,128)(2,1)S(1)} %get-tuple-element.60), channel_id=1, source_target_pairs={{0,14},{1,15},{2,0},{3,1},{4,2},{5,3},{6,4},{7,5},{8,6},{9,7},{10,... | collective-permute-start | bytes 393224 | tf_op jit(solution)/shard_map/ppermute | solution.py:14
  117.7 15.0 %collective-permute-start.9 = (bf16[128,1024]{1,0:T(8,128)(2,1)S(1)}, bf16[128,1024]{1,0:T(8,128)(2,1)S(1)}, u32[]{:S(2)}, u32[]{:S(2)}) collective-permute-start(bf16[128,1024]{1,0:T(8,128)(2,1)S(1)} %pad_maximum_fusion), channel_id=1, source_target_pairs={{0,2},{1,3},{2,4},{3,5},{4,6},{5,7},{6,8},{7,9},{8,10},{9,11},{10,... | collective-permute-start | bytes 786440 | tf_op jit(solution)/shard_map/ppermute | solution.py:14
  123.4 14.1 %collective-permute-start.11 = (bf16[128,1024]{1,0:T(8,128)(2,1)S(1)}, bf16[128,1024]{1,0:T(8,128)(2,1)S(1)}, u32[]{:S(2)}, u32[]{:S(2)}) collective-permute-start(bf16[128,1024]{1,0:T(8,128)(2,1)S(1)} %pad_maximum_fusion.1), channel_id=1, source_target_pairs={{0,14},{1,15},{2,0},{3,1},{4,2},{5,3},{6,4},{7,5},{8,6},{9,7},{10,... | collective-permute-start | bytes 786440 | tf_op jit(solution)/shard_map/ppermute | solution.py:14
  125.4 17.8 %copy-start.8 = (bf16[1,128,1024]{2,1,0:T(8,128)(2,1)S(1)}, bf16[1,128,1024]{2,1,0:T(8,128)(2,1)}, u32[]{:S(2)}) copy-start(bf16[1,128,1024]{2,1,0:T(8,128)(2,1)} %param.5) | copy-start | bytes 786436
  125.4 17.8 %collective-permute-start.13 = (bf16[128,1024]{1,0:T(8,128)(2,1)S(1)}, bf16[128,1024]{1,0:T(8,128)(2,1)S(1)}, u32[]{:S(2)}, u32[]{:S(2)}) collective-permute-start(bf16[128,1024]{1,0:T(8,128)(2,1)S(1)} %get-tuple-element.68), channel_id=1, source_target_pairs={{0,2},{1,3},{2,4},{3,5},{4,6},{5,7},{6,8},{7,9},{8,10},{9,11},{10,... | collective-permute-start | bytes 786440 | tf_op jit(solution)/shard_map/ppermute | solution.py:14
  129.5 13.7 %collective-permute-start.14 = (bf16[128,1024]{1,0:T(8,128)(2,1)S(1)}, bf16[128,1024]{1,0:T(8,128)(2,1)S(1)}, u32[]{:S(2)}, u32[]{:S(2)}) collective-permute-start(bf16[128,1024]{1,0:T(8,128)(2,1)S(1)} %get-tuple-element.69), channel_id=1, source_target_pairs={{0,14},{1,15},{2,0},{3,1},{4,2},{5,3},{6,4},{7,5},{8,6},{9,7},{10,... | collective-permute-start | bytes 786440 | tf_op jit(solution)/shard_map/ppermute | solution.py:14
  132.7 19.0 %collective-permute-start.10 = (bf16[128,1024]{1,0:T(8,128)(2,1)S(1)}, bf16[128,1024]{1,0:T(8,128)(2,1)S(1)}, u32[]{:S(2)}, u32[]{:S(2)}) collective-permute-start(bf16[128,1024]{1,0:T(8,128)(2,1)S(1)} %add_convert_fusion.2), channel_id=1, source_target_pairs={{0,20},{1,21},{2,22},{3,23},{4,24},{5,25},{6,26},{7,27},{8,28},{9,... | collective-permute-start | bytes 786440 | tf_op jit(solution)/shard_map/ppermute | solution.py:28
  137.6 21.7 %collective-permute-start.12 = (bf16[128,1024]{1,0:T(8,128)(2,1)S(1)}, bf16[128,1024]{1,0:T(8,128)(2,1)S(1)}, u32[]{:S(2)}, u32[]{:S(2)}) collective-permute-start(bf16[128,1024]{1,0:T(8,128)(2,1)S(1)} %add_convert_fusion.1), channel_id=1, source_target_pairs={{0,28},{1,29},{2,30},{3,31},{4,16},{5,17},{6,18},{7,19},{8,20},{9,... | collective-permute-start | bytes 786440 | tf_op jit(solution)/shard_map/ppermute | solution.py:28
  143.4 17.5 %collective-permute-start.15 = (bf16[128,1024]{1,0:T(8,128)(2,1)S(1)}, bf16[128,1024]{1,0:T(8,128)(2,1)S(1)}, u32[]{:S(2)}, u32[]{:S(2)}) collective-permute-start(bf16[128,1024]{1,0:T(8,128)(2,1)S(1)} %fusion.2), channel_id=1, source_target_pairs={{0,16},{1,17},{2,18},{3,19},{4,20},{5,21},{6,22},{7,23},{8,24},{9,... | collective-permute-start | bytes 786440 | tf_op jit(solution)/shard_map/ppermute | solution.py:28
Sparse Core Ops, SparseCore 0:
  10.1 75.6 all-gather.2

commit v4 on v3

--- a/solution.py
+++ b/solution.py
@@ -71,7 +71,7 @@
         put(kept_down, sent_down, pl.ds(0, units))
 
 
-def blend_kernel(upper, members, x, own, other, merged, blend_out, sums, count):
+def blend_kernel(upper, members, x, own, other, merged, blend_out, parts_out, sums, count):
     step = pl.program_id(0)
     units = sums.shape[1]
     lanes = sums.shape[2]
@@ -112,6 +112,10 @@
         root_high = jnp.sqrt(energy_high + EPS)
         blend = root_low / (root_low + agreement * root_high)
         blend_out[...] = jnp.broadcast_to(blend, blend_out.shape)
+        high = blend.astype(jnp.bfloat16)
+        low = (blend - high.astype(jnp.float32)).astype(jnp.bfloat16)
+        parts_out[:, :lanes] = jnp.broadcast_to(high, blend_out.shape)
+        parts_out[:, lanes:] = jnp.broadcast_to(low, blend_out.shape)
         for part in range(2):
             at = pl.ds(part * units, units)
             merged[at, :] = merge(is_upper, blend, own[at, :], other[at, :])
@@ -134,18 +138,20 @@
 
 def first_kernel(
     places, upper, weight_a, weight_b, weight_c, weight_d, x_a, x_b, x_c, x_d, merged_in, own_down, other_down,
-    next_own, next_other, next_own_down, next_down, blend, next_blend, term_a, term_b, term_c, term_d, term_e, gate, up, down
+    next_own, next_other, next_own_down, next_down, blend, term_a, term_b, term_c, term_d, term_e, gate, up, down
 ):
     units = blend.shape[0]
     is_upper = upper[0] == 1
     mine = blend[:, :1]
-    theirs = next_blend[:, :1]
+    features = own_down.shape[1]
+    high, low = next_down[:, features : features + 1], next_down[:, features + 128 : features + 129]
+    theirs = high.astype(jnp.float32) + low.astype(jnp.float32)
     gate[:units] = merged_in[:units]
     up[:units] = merged_in[units:]
     down[:units] = merge(is_upper, mine, own_down[...], other_down[...])
     gate[units:] = merge(is_upper, theirs, next_own[:units], next_other[:units])
     up[units:] = merge(is_upper, theirs, next_own[units:], next_other[units:])
-    down[units:] = merge(is_upper, theirs, next_own_down[...], next_down[...])
+    down[units:] = merge(is_upper, theirs, next_own_down[...], next_down[:, :features])
     weighted_terms(gate, up, down, (x_a, x_b), (weight_a, weight_b), (term_a, term_b, term_c))
     weighted_terms(gate, up, down, (x_c, x_d), (weight_c, weight_d), (term_d, term_e))
 
@@ -215,7 +221,7 @@
     held = pl.BlockSpec(memory_space=pltpu.VMEM)
     total = x_all.shape[0]
     group = 4 * rows
-    merged_in, blend = pl.pallas_call(
+    merged_in, blend, blend_parts = pl.pallas_call(
         blend_kernel,
         grid_spec=pltpu.PrefetchScalarGridSpec(
             num_scalar_prefetch=1,
@@ -226,21 +232,19 @@
                 whole((2 * units, features)),
                 whole((2 * units, features)),
             ],
-            out_specs=[whole((2 * units, features)), whole((units, 128))],
+            out_specs=[whole((2 * units, features)), whole((units, 128)), whole((units, 256))],
             scratch_shapes=[pltpu.VMEM((3, units, 128), jnp.float32), pltpu.VMEM((1, 128), jnp.float32)],
         ),
         out_shape=[
             jax.ShapeDtypeStruct((2 * units, features), jnp.bfloat16),
             jax.ShapeDtypeStruct((units, 128), jnp.float32),
+            jax.ShapeDtypeStruct((units, 256), jnp.bfloat16),
         ],
         compiler_params=pltpu.CompilerParams(vmem_limit_bytes=32 << 20),
         cost_estimate=pl.CostEstimate(flops=8 * total * units * features, bytes_accessed=2 * total * features, transcendentals=0),
         name="blend",
     )(upper, member, x_all, mine_in, partner_in)
-    next_blend = along(blend, count, sibling)
-    partner_down, blend = lax.optimization_barrier((partner_down, blend))
-    next_down = along(partner_down, count, sibling)
-
+    next_down = along(jnp.concatenate([partner_down, blend_parts], axis=1), count, sibling)
     weight_spec = lambda k: pl.BlockSpec((1, CORES, rows), lambda i, place, *_: (place[2 * i + k], 0, 0))
     x_spec = lambda k: pl.BlockSpec((rows, features), lambda i, place, *_: (place[2 * i + k], 0))
     blocks_in = lambda number: [weight_spec(k) for k in range(number)] + [x_spec(k) for k in range(number)]
@@ -254,7 +258,7 @@
             grid=(1,),
             in_specs=[
                 *blocks_in(4),
-                *[held] * 9,
+                *[held] * 8,
             ],
             out_specs=[whole(part.shape)] * 2 + [whole(block.shape)] * 3 + [whole(both)] * 3,
         ),
@@ -263,7 +267,7 @@
         cost_estimate=pl.CostEstimate(flops=24 * rows * units * features, bytes_accessed=20 * units * features, transcendentals=0),
         name="first",
     )(first_places, upper, *[row_weight] * 4, *[x_all] * 4, merged_in, mine_down, partner_down,
-      next_own, next_other, next_own_down, next_down, blend, next_blend)
+      next_own, next_other, next_own_down, next_down, blend)
     others = pl.pallas_call(
         terms_kernel,
         grid_spec=pltpu.PrefetchScalarGridSpec(

time: 171 us -> 169 us (0.988)
  waiting for transfers between devices: 64 us -> 61.4 us
    ppermute x3, starting transfers between devices: 13.8 us -> 17.4 us  [next_layer(): return lax.ppermute(array, ('section', 'expert'), route)]
    ppermute x3, waiting for transfers between devices: 12.9 us -> 9.69 us  [next_layer(): return lax.ppermute(array, ('section', 'expert'), route)]
    ppermute x13 -> x12, starting transfers between devices: 52.4 us -> 50.2 us  [along(): return lax.ppermute(array, 'expert', [(i, target(i)) for i in range(count)])]
    ppermute x13 -> x12, waiting for transfers between devices: 34.9 us -> 35.6 us  [along(): return lax.ppermute(array, 'expert', [(i, target(i)) for i in range(count)])]
  transfers between devices with their start and end apart: 17 -> 16, of which waited for: 7 -> 7; matrix products, arithmetic and copies ran while one was open for 1% -> 1% of each run, Pallas kernels for 6% -> 6%
where the time goes in v4:
time: 169 us; the launch traced here: 167 us
  starting transfers between devices  67.6 us (40%)
  waiting for transfers between devices  61.4 us (36%)
  between operations  14.5 us (9%)
  Pallas kernels  12.6 us (7%)
  local copies, waits for them, and re-layouts  8.83 us (5%)
  other arithmetic  2.52 us (1%)
    ppermute x12, starting transfers between devices, along(): return lax.ppermute(array, 'expert', [(i, target(i)) for i in range(count)])  50.2 us
    ppermute x12, waiting for transfers between devices, along(): return lax.ppermute(array, 'expert', [(i, target(i)) for i in range(count)])  35.6 us
    ppermute x3, starting transfers between devices, next_layer(): return lax.ppermute(array, ('section', 'expert'), route)  17.4 us
    all_gather x1, waiting for transfers between devices, local(): x_all = lax.all_gather(x_local, 'expert', axis=0, tiled=True)  15.5 us
    ppermute x3, waiting for transfers between devices, next_layer(): return lax.ppermute(array, ('section', 'expert'), route)  9.69 us
    unnamed x24, local copies, waits for them, and re-layouts  8.66 us
    pallas_call x1, Pallas kernels, local(): pl.pallas_call(blend_kernel, grid_spec=pltpu.PrefetchScalarGridSpec(num_s...  5.41 us
  transfers between devices with their start and end apart: 16, of which 7 were waited for; matrix products, arithmetic and copies ran while one was open for 1% of the time, Pallas kernels for 6%

profile of v4, /device:TPU:6, one launch (start us, length us, event | category | flops | bytes accessed | tf_op | source)
XLA Modules:
  0.0 167.4 jit_solution(423128545749278628)
XLA Ops:
  7.2 0.0 all-gather.3.cloned.1.call-start
  7.2 0.7 all-gather.3.cloned.1.call-update
  7.9 0.0 copy-start.2
  7.9 1.7 copy-done.2
  9.6 0.0 copy-start.9
  9.6 0.0 copy-start.10
  9.6 0.0 copy-start.11
  9.6 1.9 %split.1 = (bf16[384,1024]{1,0:T(8,128)(2,1)S(1)}, bf16[192,1024]{1,0:T(8,128)(2,1)S(1)}, bf16[384,1024]{1,0:T(8,128)(2,1)}, bf16[192,1024]{1,0:T(8,128)(2,1)S(1)}) custom-call(s32[1]{0:T(128)} %bitcast.3.upper, bf16[3,1024,384]{2,1,0:T(8,128)(2,1)S(1)} %bitcast.28), custom_call_target="tpu_custom_call" | custom-call | bytes 4718592 | tf_op jit(solution)/shard_map/split/pallas_call | solution.py:187
  11.4 0.0 copy-start.7
  11.4 0.8 copy-done.7
  12.2 10.9 %collective-permute-start = (bf16[384,1024]{1,0:T(8,128)(2,1)}, bf16[384,1024]{1,0:T(8,128)(2,1)S(1)}, u32[]{:S(2)}, u32[]{:S(2)}) collective-permute-start(bf16[384,1024]{1,0:T(8,128)(2,1)} %get-tuple-element.41), channel_id=1, source_target_pairs={{0,8},{1,9},{2,10},{3,11},{4,12},{5,13},{6,14},{7,15},{8,0},{9,1},... | collective-permute-start | bytes 2359304 | tf_op jit(solution)/shard_map/ppermute | solution.py:14
  23.1 0.0 copy-done.9
  23.2 0.0 copy-done.10
  23.2 0.1 select_reduce_fusion.1
  23.2 0.0 copy-done.11
  23.3 0.1 fusion.7
  23.4 1.9 %collective-permute-start.2 = (bf16[384,1024]{1,0:T(8,128)(2,1)S(1)}, bf16[384,1024]{1,0:T(8,128)(2,1)S(1)}, u32[]{:S(2)}, u32[]{:S(2)}) collective-permute-start(bf16[384,1024]{1,0:T(8,128)(2,1)S(1)} %get-tuple-element.45.own), channel_id=1, source_target_pairs={{0,1},{1,0},{2,3},{3,2},{4,5},{5,4},{6,7},{7,6},{8,9},{9,8},{10,11... | collective-permute-start | bytes 2359304 | tf_op jit(solution)/shard_map/ppermute | solution.py:14
  25.3 0.0 copy-start.5
  25.3 0.9 copy-done.5
  26.2 2.4 %collective-permute-start.3 = (bf16[192,1024]{1,0:T(8,128)(2,1)S(1)}, bf16[192,1024]{1,0:T(8,128)(2,1)S(1)}, u32[]{:S(2)}, u32[]{:S(2)}) collective-permute-start(bf16[192,1024]{1,0:T(8,128)(2,1)S(1)} %get-tuple-element.46.own_down), channel_id=1, source_target_pairs={{0,1},{1,0},{2,3},{3,2},{4,5},{5,4},{6,7},{7,6},{8,9},{9,8},{10,11... | collective-permute-start | bytes 1179656 | tf_op jit(solution)/shard_map/ppermute | solution.py:14
  28.6 29.9 %collective-permute-done.other = bf16[384,1024]{1,0:T(8,128)(2,1)S(1)} collective-permute-done((bf16[384,1024]{1,0:T(8,128)(2,1)}, bf16[384,1024]{1,0:T(8,128)(2,1)S(1)}, u32[]{:S(2)}, u32[]{:S(2)}) %collective-permute-start) | collective-permute-done | bytes 786464 | tf_op jit(solution)/shard_map/ppermute | solution.py:14
  58.4 0.9 copy-done.3
  59.3 9.0 %collective-permute-start.1 = (bf16[192,1024]{1,0:T(8,128)(2,1)}, bf16[192,1024]{1,0:T(8,128)(2,1)S(1)}, u32[]{:S(2)}, u32[]{:S(2)}) collective-permute-start(bf16[192,1024]{1,0:T(8,128)(2,1)} %copy-done.7), channel_id=1, source_target_pairs={{0,8},{1,9},{2,10},{3,11},{4,12},{5,13},{6,14},{7,15},{8,0},{9,1},... | collective-permute-start | bytes 1179656 | tf_op jit(solution)/shard_map/ppermute | solution.py:14
  68.4 0.0 collective-permute-done.3.next_own_down
  68.4 0.0 collective-permute-done.2.next_own
  68.4 1.9 %collective-permute-start.4 = (bf16[384,1024]{1,0:T(8,128)(2,1)}, bf16[384,1024]{1,0:T(8,128)(2,1)S(1)}, u32[]{:S(2)}, u32[]{:S(2)}) collective-permute-start(bf16[384,1024]{1,0:T(8,128)(2,1)} %copy-done.3), channel_id=1, source_target_pairs={{0,1},{1,0},{2,3},{3,2},{4,5},{5,4},{6,7},{7,6},{8,9},{9,8},{10,11... | collective-permute-start | bytes 2359304 | tf_op jit(solution)/shard_map/ppermute | solution.py:14
  70.3 15.5 %all-gather.3.cloned.1.call-done = bf16[1,2048,1024]{2,1,0:T(8,128)(2,1)} async-done(((bf16[1,128,1024]{2,1,0:T(8,128)(2,1)}), bf16[1,2048,1024]{2,1,0:T(8,128)(2,1)}) %all-gather.3.cloned.1.call-update) | async-done | bytes 4194320 | tf_op jit(solution)/shard_map/all_gather | solution.py:184
  85.8 2.2 %copy-done = bf16[1,2048,1024]{2,1,0:T(8,128)(2,1)S(1)} copy-done((bf16[1,2048,1024]{2,1,0:T(8,128)(2,1)S(1)}, bf16[1,2048,1024]{2,1,0:T(8,128)(2,1)}, u32[]{:S(2)}) %copy-start) | copy-done | bytes 4194328
  88.0 1.1 copy-done.4
  89.1 1.1 copy-done.6
  90.2 5.4 %blend.1 = (bf16[384,1024]{1,0:T(8,128)(2,1)S(1)}, f32[192,128]{1,0:T(8,128)S(1)}, bf16[192,256]{1,0:T(8,128)(2,1)S(1)}) custom-call(s32[1]{0:T(128)} %bitcast.3.upper, f32[4,1,512]{2,1,0:T(1,128)S(1)} %bitcast.29, bf16[2048,1024]{1,0:T(8,128)(2,1)S(1)} %bitcast.21, bf16[384,1024]{1,0:T(8,128)(2,1)S(1)} %copy-done.6, bf16[384,1024]{1,0:T(8,128)(2,1)S(1)} %copy-done.4), custom_call_target="tpu_custom_call" | custom-call | flops 3221225472 | bytes 4194304 | tf_op jit(solution)/shard_map/blend/pallas_call | solution.py:224
  95.6 0.0 collective-permute-done.1.other_down
  95.7 2.1 %collective-permute-start.5 = (bf16[192,1280]{1,0:T(8,128)(2,1)S(1)}, bf16[192,1280]{1,0:T(8,128)(2,1)S(1)}, u32[]{:S(2)}, u32[]{:S(2)}) collective-permute-start(bf16[192,1280]{1,0:T(8,128)(2,1)S(1)} %pad_maximum_fusion), channel_id=1, source_target_pairs={{0,1},{1,0},{2,3},{3,2},{4,5},{5,4},{6,7},{7,6},{8,9},{9,8},{10,11... | collective-permute-start | bytes 1474568 | tf_op jit(solution)/shard_map/ppermute | solution.py:14
  97.9 0.0 collective-permute-done.4.next_other
  97.9 1.6 collective-permute-done.5.next_down
  99.5 0.0 copy-done.1
  99.5 2.6 %first.1 = (bf16[64,1024]{1,0:T(8,128)(2,1)S(1)}, bf16[64,1024]{1,0:T(8,128)(2,1)S(1)}, bf16[128,1024]{1,0:T(8,128)(2,1)S(1)}, bf16[128,1024]{1,0:T(8,128)(2,1)S...) custom-call(s32[4]{0:T(128)S(1)} %get-tuple-element.37.places, ...), custom_call_target="tpu_custom_call" | custom-call | flops 603979776 | bytes 3932160 | tf_op jit(solution)/shard_map/first/pallas_call | solution.py:254
  102.1 5.1 %collective-permute-start.6 = (bf16[64,1024]{1,0:T(8,128)(2,1)S(1)}, bf16[64,1024]{1,0:T(8,128)(2,1)S(1)}, u32[]{:S(2)}, u32[]{:S(2)}) collective-permute-start(bf16[64,1024]{1,0:T(8,128)(2,1)S(1)} %get-tuple-element.55), channel_id=1, source_target_pairs={{0,2},{1,3},{2,4},{3,5},{4,6},{5,7},{6,8},{7,9},{8,10},{9,11},{10,... | collective-permute-start | bytes 393224 | tf_op jit(solution)/shard_map/ppermute | solution.py:14
  107.2 2.0 %collective-permute-start.7 = (bf16[64,1024]{1,0:T(8,128)(2,1)S(1)}, bf16[64,1024]{1,0:T(8,128)(2,1)S(1)}, u32[]{:S(2)}, u32[]{:S(2)}) collective-permute-start(bf16[64,1024]{1,0:T(8,128)(2,1)S(1)} %get-tuple-element.58), channel_id=1, source_target_pairs={{0,14},{1,15},{2,0},{3,1},{4,2},{5,3},{6,4},{7,5},{8,6},{9,7},{10,... | collective-permute-start | bytes 393224 | tf_op jit(solution)/shard_map/ppermute | solution.py:14
  109.2 2.7 %terms.1 = (bf16[128,1024]{1,0:T(8,128)(2,1)S(1)}, bf16[128,1024]{1,0:T(8,128)(2,1)S(1)}, bf16[128,1024]{1,0:T(8,128)(2,1)S(1)}, bf16[128,1024]{1,0:T(8,128)(2,1)S(1)}) custom-call(s32[4]{0:T(128)S(1)} %get-tuple-element.59.places, f32[16,2,128]{2,1,0:T(2,128)S(1)} %pad_maximum_fusion.3.weight_a.weight_b.weight_c.weight_d, ...), custom_call_target="tpu_custom_call" | custom-call | flops 603979776 | bytes 4194304 | tf_op jit(solution)/shard_map/terms/pallas_call | solution.py:271
  111.9 0.0 collective-permute-done.6
  112.0 4.1 %collective-permute-done.7 = bf16[64,1024]{1,0:T(8,128)(2,1)S(1)} collective-permute-done((bf16[64,1024]{1,0:T(8,128)(2,1)S(1)}, bf16[64,1024]{1,0:T(8,128)(2,1)S(1)}, u32[]{:S(2)}, u32[]{:S(2)}) %collective-permute-start.7) | collective-permute-done | bytes 131104 | tf_op jit(solution)/shard_map/ppermute | solution.py:14
  116.2 5.7 %collective-permute-start.8 = (bf16[128,1024]{1,0:T(8,128)(2,1)S(1)}, bf16[128,1024]{1,0:T(8,128)(2,1)S(1)}, u32[]{:S(2)}, u32[]{:S(2)}) collective-permute-start(bf16[128,1024]{1,0:T(8,128)(2,1)S(1)} %pad_maximum_fusion.1), channel_id=1, source_target_pairs={{0,2},{1,3},{2,4},{3,5},{4,6},{5,7},{6,8},{7,9},{8,10},{9,11},{10,... | collective-permute-start | bytes 786440 | tf_op jit(solution)/shard_map/ppermute | solution.py:14
  121.9 1.9 %collective-permute-start.10 = (bf16[128,1024]{1,0:T(8,128)(2,1)S(1)}, bf16[128,1024]{1,0:T(8,128)(2,1)S(1)}, u32[]{:S(2)}, u32[]{:S(2)}) collective-permute-start(bf16[128,1024]{1,0:T(8,128)(2,1)S(1)} %pad_maximum_fusion.2), channel_id=1, source_target_pairs={{0,14},{1,15},{2,0},{3,1},{4,2},{5,3},{6,4},{7,5},{8,6},{9,7},{10,... | collective-permute-start | bytes 786440 | tf_op jit(solution)/shard_map/ppermute | solution.py:14
  123.8 0.1 slice_bitcast_fusion
  123.9 0.0 copy-start.8
  123.9 4.1 %collective-permute-start.12 = (bf16[128,1024]{1,0:T(8,128)(2,1)S(1)}, bf16[128,1024]{1,0:T(8,128)(2,1)S(1)}, u32[]{:S(2)}, u32[]{:S(2)}) collective-permute-start(bf16[128,1024]{1,0:T(8,128)(2,1)S(1)} %get-tuple-element.66), channel_id=1, source_target_pairs={{0,2},{1,3},{2,4},{3,5},{4,6},{5,7},{6,8},{7,9},{8,10},{9,11},{10,... | collective-permute-start | bytes 786440 | tf_op jit(solution)/shard_map/ppermute | solution.py:14
  128.0 3.1 %collective-permute-start.13 = (bf16[128,1024]{1,0:T(8,128)(2,1)S(1)}, bf16[128,1024]{1,0:T(8,128)(2,1)S(1)}, u32[]{:S(2)}, u32[]{:S(2)}) collective-permute-start(bf16[128,1024]{1,0:T(8,128)(2,1)S(1)} %get-tuple-element.67), channel_id=1, source_target_pairs={{0,14},{1,15},{2,0},{3,1},{4,2},{5,3},{6,4},{7,5},{8,6},{9,7},{10,... | collective-permute-start | bytes 786440 | tf_op jit(solution)/shard_map/ppermute | solution.py:14
  131.1 0.0 collective-permute-done.8
  131.1 0.1 add_convert_fusion.2
  131.2 4.7 %collective-permute-start.9 = (bf16[128,1024]{1,0:T(8,128)(2,1)S(1)}, bf16[128,1024]{1,0:T(8,128)(2,1)S(1)}, u32[]{:S(2)}, u32[]{:S(2)}) collective-permute-start(bf16[128,1024]{1,0:T(8,128)(2,1)S(1)} %add_convert_fusion.2), channel_id=1, source_target_pairs={{0,20},{1,21},{2,22},{3,23},{4,24},{5,25},{6,26},{7,27},{8,28},{9,... | collective-permute-start | bytes 786440 | tf_op jit(solution)/shard_map/ppermute | solution.py:28
  135.8 0.0 collective-permute-done.10
  135.9 0.1 add_convert_fusion.1
  135.9 10.8 %collective-permute-start.11 = (bf16[128,1024]{1,0:T(8,128)(2,1)S(1)}, bf16[128,1024]{1,0:T(8,128)(2,1)S(1)}, u32[]{:S(2)}, u32[]{:S(2)}) collective-permute-start(bf16[128,1024]{1,0:T(8,128)(2,1)S(1)} %add_convert_fusion.1), channel_id=1, source_target_pairs={{0,28},{1,29},{2,30},{3,31},{4,16},{5,17},{6,18},{7,19},{8,20},{9,... | collective-permute-start | bytes 786440 | tf_op jit(solution)/shard_map/ppermute | solution.py:28
  146.7 0.0 collective-permute-done.12
  146.7 0.0 collective-permute-done.13
  146.7 0.0 copy-done.8
  146.8 0.2 fusion.2
  146.9 1.9 %collective-permute-start.14 = (bf16[128,1024]{1,0:T(8,128)(2,1)S(1)}, bf16[128,1024]{1,0:T(8,128)(2,1)S(1)}, u32[]{:S(2)}, u32[]{:S(2)}) collective-permute-start(bf16[128,1024]{1,0:T(8,128)(2,1)S(1)} %fusion.2), channel_id=1, source_target_pairs={{0,16},{1,17},{2,18},{3,19},{4,20},{5,21},{6,22},{7,23},{8,24},{9,... | collective-permute-start | bytes 786440 | tf_op jit(solution)/shard_map/ppermute | solution.py:28
  148.9 1.1 maximum_bitcast_fusion
  150.0 0.1 collective-permute-done.9
  150.1 6.9 %collective-permute-done.11 = bf16[128,1024]{1,0:T(8,128)(2,1)S(1)} collective-permute-done((bf16[128,1024]{1,0:T(8,128)(2,1)S(1)}, bf16[128,1024]{1,0:T(8,128)(2,1)S(1)}, u32[]{:S(2)}, u32[]{:S(2)}) %collective-permute-start.11) | collective-permute-done | bytes 262176 | tf_op jit(solution)/shard_map/ppermute | solution.py:28
  157.0 2.7 %collective-permute-done.14 = bf16[128,1024]{1,0:T(8,128)(2,1)S(1)} collective-permute-done((bf16[128,1024]{1,0:T(8,128)(2,1)S(1)}, bf16[128,1024]{1,0:T(8,128)(2,1)S(1)}, u32[]{:S(2)}, u32[]{:S(2)}) %collective-permute-start.14) | collective-permute-done | bytes 262176 | tf_op jit(solution)/shard_map/ppermute | solution.py:28
  159.7 0.8 fusion.3
  (15 shorter events, 0.2 us)
Async XLA Ops:
  7.2 78.6 %all-gather.3.cloned.1.call-start = ((), (), s32[]{:S(2)}) async-start(), calls=%async_computation | async-start | bytes 4456448 | tf_op jit(solution)/shard_map/all_gather | solution.py:184
  7.9 1.7 copy-start.2
  9.6 13.6 %copy-start.9 = (f32[1,2048,8]{1,2,0:T(8,128)S(1)}, f32[1,2048,8]{1,2,0:T(8,128)}, u32[]{:S(2)}) copy-start(f32[1,2048,8]{1,2,0:T(8,128)} %param.7) | copy-start | bytes 196612
  9.6 13.6 %copy-start.10 = (s32[1,2048,8]{1,2,0:T(8,128)S(1)}, s32[1,2048,8]{1,2,0:T(8,128)}, u32[]{:S(2)}) copy-start(s32[1,2048,8]{1,2,0:T(8,128)} %param.6) | copy-start | bytes 196612
  9.6 13.7 %copy-start.11 = (s32[8]{0:T(128)S(1)}, s32[8]{0:T(128)}, u32[]{:S(2)}) copy-start(s32[8]{0:T(128)} %constant.54.clone) | copy-start | bytes 100
  11.4 0.8 copy-start.7
  12.2 46.2 %collective-permute-start = (bf16[384,1024]{1,0:T(8,128)(2,1)}, bf16[384,1024]{1,0:T(8,128)(2,1)S(1)}, u32[]{:S(2)}, u32[]{:S(2)}) collective-permute-start(bf16[384,1024]{1,0:T(8,128)(2,1)} %get-tuple-element.41), channel_id=1, source_target_pairs={{0,8},{1,9},{2,10},{3,11},{4,12},{5,13},{6,14},{7,15},{8,0},{9,1},... | collective-permute-start | bytes 2359304 | tf_op jit(solution)/shard_map/ppermute | solution.py:14
  23.4 45.0 %collective-permute-start.2 = (bf16[384,1024]{1,0:T(8,128)(2,1)S(1)}, bf16[384,1024]{1,0:T(8,128)(2,1)S(1)}, u32[]{:S(2)}, u32[]{:S(2)}) collective-permute-start(bf16[384,1024]{1,0:T(8,128)(2,1)S(1)} %get-tuple-element.45.own), channel_id=1, source_target_pairs={{0,1},{1,0},{2,3},{3,2},{4,5},{5,4},{6,7},{7,6},{8,9},{9,8},{10,11... | collective-permute-start | bytes 2359304 | tf_op jit(solution)/shard_map/ppermute | solution.py:14
  25.3 0.9 copy-start.5
  26.2 42.2 %collective-permute-start.3 = (bf16[192,1024]{1,0:T(8,128)(2,1)S(1)}, bf16[192,1024]{1,0:T(8,128)(2,1)S(1)}, u32[]{:S(2)}, u32[]{:S(2)}) collective-permute-start(bf16[192,1024]{1,0:T(8,128)(2,1)S(1)} %get-tuple-element.46.own_down), channel_id=1, source_target_pairs={{0,1},{1,0},{2,3},{3,2},{4,5},{5,4},{6,7},{7,6},{8,9},{9,8},{10,11... | collective-permute-start | bytes 1179656 | tf_op jit(solution)/shard_map/ppermute | solution.py:14
  58.4 0.9 copy-start.3
  59.3 36.3 %collective-permute-start.1 = (bf16[192,1024]{1,0:T(8,128)(2,1)}, bf16[192,1024]{1,0:T(8,128)(2,1)S(1)}, u32[]{:S(2)}, u32[]{:S(2)}) collective-permute-start(bf16[192,1024]{1,0:T(8,128)(2,1)} %copy-done.7), channel_id=1, source_target_pairs={{0,8},{1,9},{2,10},{3,11},{4,12},{5,13},{6,14},{7,15},{8,0},{9,1},... | collective-permute-start | bytes 1179656 | tf_op jit(solution)/shard_map/ppermute | solution.py:14
  68.4 29.5 %collective-permute-start.4 = (bf16[384,1024]{1,0:T(8,128)(2,1)}, bf16[384,1024]{1,0:T(8,128)(2,1)S(1)}, u32[]{:S(2)}, u32[]{:S(2)}) collective-permute-start(bf16[384,1024]{1,0:T(8,128)(2,1)} %copy-done.3), channel_id=1, source_target_pairs={{0,1},{1,0},{2,3},{3,2},{4,5},{5,4},{6,7},{7,6},{8,9},{9,8},{10,11... | collective-permute-start | bytes 2359304 | tf_op jit(solution)/shard_map/ppermute | solution.py:14
  85.8 2.2 %copy-start = (bf16[1,2048,1024]{2,1,0:T(8,128)(2,1)S(1)}, bf16[1,2048,1024]{2,1,0:T(8,128)(2,1)}, u32[]{:S(2)}) copy-start(bf16[1,2048,1024]{2,1,0:T(8,128)(2,1)} %all-gather.3.cloned.1.call-done) | copy-start | bytes 12582916
  88.0 1.1 copy-start.4
  89.1 1.1 copy-start.6
  90.2 9.2 %copy-start.1 = (bf16[1,2048,1024]{2,1,0:T(8,128)(2,1)S(1)}, bf16[1,2048,1024]{2,1,0:T(8,128)(2,1)}, u32[]{:S(2)}) copy-start(bf16[1,2048,1024]{2,1,0:T(8,128)(2,1)} %all-gather.3.cloned.1.call-done) | copy-start | bytes 12582916
  95.7 3.8 %collective-permute-start.5 = (bf16[192,1280]{1,0:T(8,128)(2,1)S(1)}, bf16[192,1280]{1,0:T(8,128)(2,1)S(1)}, u32[]{:S(2)}, u32[]{:S(2)}) collective-permute-start(bf16[192,1280]{1,0:T(8,128)(2,1)S(1)} %pad_maximum_fusion), channel_id=1, source_target_pairs={{0,1},{1,0},{2,3},{3,2},{4,5},{5,4},{6,7},{7,6},{8,9},{9,8},{10,11... | collective-permute-start | bytes 1474568 | tf_op jit(solution)/shard_map/ppermute | solution.py:14
  102.1 9.8 %collective-permute-start.6 = (bf16[64,1024]{1,0:T(8,128)(2,1)S(1)}, bf16[64,1024]{1,0:T(8,128)(2,1)S(1)}, u32[]{:S(2)}, u32[]{:S(2)}) collective-permute-start(bf16[64,1024]{1,0:T(8,128)(2,1)S(1)} %get-tuple-element.55), channel_id=1, source_target_pairs={{0,2},{1,3},{2,4},{3,5},{4,6},{5,7},{6,8},{7,9},{8,10},{9,11},{10,... | collective-permute-start | bytes 393224 | tf_op jit(solution)/shard_map/ppermute | solution.py:14
  107.2 8.9 %collective-permute-start.7 = (bf16[64,1024]{1,0:T(8,128)(2,1)S(1)}, bf16[64,1024]{1,0:T(8,128)(2,1)S(1)}, u32[]{:S(2)}, u32[]{:S(2)}) collective-permute-start(bf16[64,1024]{1,0:T(8,128)(2,1)S(1)} %get-tuple-element.58), channel_id=1, source_target_pairs={{0,14},{1,15},{2,0},{3,1},{4,2},{5,3},{6,4},{7,5},{8,6},{9,7},{10,... | collective-permute-start | bytes 393224 | tf_op jit(solution)/shard_map/ppermute | solution.py:14
  116.2 14.9 %collective-permute-start.8 = (bf16[128,1024]{1,0:T(8,128)(2,1)S(1)}, bf16[128,1024]{1,0:T(8,128)(2,1)S(1)}, u32[]{:S(2)}, u32[]{:S(2)}) collective-permute-start(bf16[128,1024]{1,0:T(8,128)(2,1)S(1)} %pad_maximum_fusion.1), channel_id=1, source_target_pairs={{0,2},{1,3},{2,4},{3,5},{4,6},{5,7},{6,8},{7,9},{8,10},{9,11},{10,... | collective-permute-start | bytes 786440 | tf_op jit(solution)/shard_map/ppermute | solution.py:14
  121.9 14.0 %collective-permute-start.10 = (bf16[128,1024]{1,0:T(8,128)(2,1)S(1)}, bf16[128,1024]{1,0:T(8,128)(2,1)S(1)}, u32[]{:S(2)}, u32[]{:S(2)}) collective-permute-start(bf16[128,1024]{1,0:T(8,128)(2,1)S(1)} %pad_maximum_fusion.2), channel_id=1, source_target_pairs={{0,14},{1,15},{2,0},{3,1},{4,2},{5,3},{6,4},{7,5},{8,6},{9,7},{10,... | collective-permute-start | bytes 786440 | tf_op jit(solution)/shard_map/ppermute | solution.py:14
  123.9 22.9 %copy-start.8 = (bf16[1,128,1024]{2,1,0:T(8,128)(2,1)S(1)}, bf16[1,128,1024]{2,1,0:T(8,128)(2,1)}, u32[]{:S(2)}) copy-start(bf16[1,128,1024]{2,1,0:T(8,128)(2,1)} %param.5) | copy-start | bytes 786436
  123.9 22.8 %collective-permute-start.12 = (bf16[128,1024]{1,0:T(8,128)(2,1)S(1)}, bf16[128,1024]{1,0:T(8,128)(2,1)S(1)}, u32[]{:S(2)}, u32[]{:S(2)}) collective-permute-start(bf16[128,1024]{1,0:T(8,128)(2,1)S(1)} %get-tuple-element.66), channel_id=1, source_target_pairs={{0,2},{1,3},{2,4},{3,5},{4,6},{5,7},{6,8},{7,9},{8,10},{9,11},{10,... | collective-permute-start | bytes 786440 | tf_op jit(solution)/shard_map/ppermute | solution.py:14
  128.0 18.8 %collective-permute-start.13 = (bf16[128,1024]{1,0:T(8,128)(2,1)S(1)}, bf16[128,1024]{1,0:T(8,128)(2,1)S(1)}, u32[]{:S(2)}, u32[]{:S(2)}) collective-permute-start(bf16[128,1024]{1,0:T(8,128)(2,1)S(1)} %get-tuple-element.67), channel_id=1, source_target_pairs={{0,14},{1,15},{2,0},{3,1},{4,2},{5,3},{6,4},{7,5},{8,6},{9,7},{10,... | collective-permute-start | bytes 786440 | tf_op jit(solution)/shard_map/ppermute | solution.py:14
  131.2 18.9 %collective-permute-start.9 = (bf16[128,1024]{1,0:T(8,128)(2,1)S(1)}, bf16[128,1024]{1,0:T(8,128)(2,1)S(1)}, u32[]{:S(2)}, u32[]{:S(2)}) collective-permute-start(bf16[128,1024]{1,0:T(8,128)(2,1)S(1)} %add_convert_fusion.2), channel_id=1, source_target_pairs={{0,20},{1,21},{2,22},{3,23},{4,24},{5,25},{6,26},{7,27},{8,28},{9,... | collective-permute-start | bytes 786440 | tf_op jit(solution)/shard_map/ppermute | solution.py:28
  135.9 21.1 %collective-permute-start.11 = (bf16[128,1024]{1,0:T(8,128)(2,1)S(1)}, bf16[128,1024]{1,0:T(8,128)(2,1)S(1)}, u32[]{:S(2)}, u32[]{:S(2)}) collective-permute-start(bf16[128,1024]{1,0:T(8,128)(2,1)S(1)} %add_convert_fusion.1), channel_id=1, source_target_pairs={{0,28},{1,29},{2,30},{3,31},{4,16},{5,17},{6,18},{7,19},{8,20},{9,... | collective-permute-start | bytes 786440 | tf_op jit(solution)/shard_map/ppermute | solution.py:28
  146.9 12.8 %collective-permute-start.14 = (bf16[128,1024]{1,0:T(8,128)(2,1)S(1)}, bf16[128,1024]{1,0:T(8,128)(2,1)S(1)}, u32[]{:S(2)}, u32[]{:S(2)}) collective-permute-start(bf16[128,1024]{1,0:T(8,128)(2,1)S(1)} %fusion.2), channel_id=1, source_target_pairs={{0,16},{1,17},{2,18},{3,19},{4,20},{5,21},{6,22},{7,23},{8,24},{9,... | collective-permute-start | bytes 786440 | tf_op jit(solution)/shard_map/ppermute | solution.py:28
Sparse Core Ops, SparseCore 0:
  10.1 75.6 all-gather.2
